TPU v7x, 32 devices: a whole 2x2x4 slice. The times are simulated.
32 devices in a mesh: grp: 2 (over y), krow: 4 (over z), exc: 2 (over x), band: 2 (over core).
Axes of the slice: x: 2, y: 2, z: 4, core: 2. Of those that a mesh axis runs over, the one named last changes fastest.
Arguments:
- coef_zero: bfloat16 [800, 4, 4, 512], P(('grp', 'exc'), None, None, 'krow'), parts along dimension 0, may hold values from -6 to 6
- coef_shift: bfloat16 [4, 800, 4, 4, 512], P(None, ('grp', 'exc'), 'band', None, 'krow'), parts along dimension 1, may hold values from -6 to 6
- coupling: bfloat16 [2, 8, 9, 4, 4, 512], P(None, 'grp', None, None, None, 'krow'), parts along dimension 1, may hold values from -6 to 6
- partner: int32 [4, 512], replicated, may hold values from 0 to 511, as said below
Outputs:
- exciton_coupling: float32 [800, 4, 9, 400], P(('grp', 'krow'), 'band', None, 'exc'), parts along dimension 0
There are 2 independent parts, one for each index of `grp`. A program takes and returns all parts, laid end to end along the dimension named above; an argument that names none is the same for every part. Nothing has to cross between parts.
Inputs may be any that keep to these rules, and one draw needn't show every extreme that they name: For every q, partner[q] is a permutation of the k points; the k points of one aligned block of 128 have their partners in exactly 4 such blocks, 32 in each.
All inputs are finite; a program needn't handle non-finite values.
Results may differ from a plain program's by a relative error of at most 0.0029.
Values may be sent and summed in bfloat16 or wider, within the bound.
A program may use at most 192 MiB of HBM per device.

v0:
```python
import jax
import jax.numpy as jnp
from jax import lax
from jax.sharding import PartitionSpec as P

PEERS = 4


def take_rows(rows, index):
    return jnp.take(rows, index, axis=-1)


def local(coef_zero, coef_shift, coupling, partner):
    nrow = lax.axis_size("krow")
    me = lax.axis_index("krow")
    nband = lax.axis_size("band")
    half = lax.axis_index("band")
    kdev = coef_zero.shape[-1]
    nq = coef_shift.shape[0]
    share = coef_shift.shape[1]
    lower = coef_shift.shape[2]
    modes = coupling.shape[2]
    cap = kdev // PEERS
    pairs = coef_zero.shape[1] * coef_zero.shape[2]
    scale = (1.0 * pairs * nrow * kdev) ** (-0.5)
    whole_zero = lax.all_gather(coef_zero, "exc", axis=0, tiled=True)
    states = whole_zero.shape[0]
    kept_rows = states // nrow
    zero_flat = whole_zero.reshape(states, -1)
    owner = (partner // kdev).reshape(nq, nrow, kdev)
    within = (partner % kdev).reshape(nq, nrow, kdev)
    flags = (owner == me).astype(jnp.int32)
    ranks = jnp.cumsum(flags, axis=-1) - 1
    slots = jnp.arange(cap, dtype=jnp.int32)
    picked = (flags[..., None] == 1) & (ranks[..., None] == slots)
    send_index = jnp.sum(jnp.where(picked, within[..., None], 0), axis=2).reshape(nq, nrow * cap)
    outgoing = jax.vmap(take_rows)(coef_shift, send_index)
    incoming = lax.all_to_all(outgoing, "krow", split_axis=4, concat_axis=4, tiled=True)
    my_owner = lax.dynamic_index_in_dim(owner, me, axis=1, keepdims=False)
    peers_ids = jnp.arange(nrow, dtype=jnp.int32)
    match = (my_owner[..., None] == peers_ids).astype(jnp.int32)
    before = jnp.cumsum(match, axis=1) - 1
    my_rank = jnp.sum(match * before, axis=-1)
    shifted = jax.vmap(take_rows)(incoming, my_owner * cap + my_rank)

    def contract(table, rows):
        return lax.dot_general(
            rows, table, (((1,), (1,)), ((), ())), preferred_element_type=jnp.float32
        )

    pieces = []
    groups = nq // nband
    full_coef, full_shifted = (
        lax.all_to_all(coef_shift, "band", split_axis=0, concat_axis=2, tiled=True),
        lax.all_to_all(shifted, "band", split_axis=0, concat_axis=2, tiled=True),
    )
    valence = full_coef.shape[2]
    band_ids = jnp.arange(valence, dtype=jnp.int32) // lower
    for group in range(groups):
        q_index = half * groups + group
        couple_q = lax.dynamic_index_in_dim(coupling, q_index, axis=1, keepdims=False)
        elec = jnp.einsum(
            "svak,mack->msvck", full_shifted[group], couple_q[0], preferred_element_type=jnp.float32
        )
        tables = []
        for h in range(nband):
            coef_part = full_coef[group][:, h * lower : (h + 1) * lower]
            hole_table = couple_q[1][:, :, h * lower : (h + 1) * lower]
            hole = jnp.einsum(
                "swck,mvwk->msvck", coef_part, hole_table, preferred_element_type=jnp.float32
            )
            inside = (band_ids == h)[None, None, :, None, None]
            table_h = (jnp.where(inside, elec, 0.0) - hole).astype(jnp.bfloat16)
            tables.append(table_h.reshape(modes * share, -1))
        stacked_tables = jnp.stack(tables, axis=0)
        total = contract(stacked_tables[0], zero_flat)
        total = total + contract(stacked_tables[1], zero_flat)
        pieces.append(
            lax.psum_scatter(
                (total * scale).reshape(lax.axis_size("krow") * kept_rows, modes, share),
                "krow",
                scatter_dimension=0,
                tiled=True,
            )
        )
    result = jnp.stack(pieces, axis=1)
    return result


def solution(mesh):
    placed = (
        P(("grp", "exc"), None, None, "krow"),
        P(None, ("grp", "exc"), "band", None, "krow"),
        P(None, "grp", None, None, None, "krow"),
        P(),
    )
    return jax.shard_map(
        local,
        mesh=mesh,
        in_specs=placed,
        out_specs=P(("grp", "krow"), "band", None, "exc"),
        check_vma=False,
    )
```

profile of v0, /device:TPU:0, one launch (start us, length us, event | category | flops | bytes accessed | tf_op | source)
XLA Modules:
  0.0 659.9 jit_solution(13809634621076966063)
XLA Ops:
  9.3 4.8 all-to-all-start.2
  14.1 5.1 copy.116
  21.8 6.4 gather_fusion
  28.3 3.5 fusion.4
  31.7 6.3 all-to-all-start
  57.5 12.4 %all-gather.2.cloned.1.call-done = bf16[400,4,4,128]{3,2,1,0:T(4,128)(2,1)} async-done(((bf16[200,4,4,128]{3,2,1,0:T(4,128)(2,1)}), bf16[400,4,4,128]{3,2,1,0:T(4,128)(2,1)}) %all-gather.2.cloned.1.call-update) | async-done | bytes 1638416 | tf_op jit(solution)/shard_map/all_gather | solution.py:26
  69.8 3.9 reshape.78
  73.7 13.1 %all-to-all-done = bf16[4,200,2,4,128]{1,3,2,0,4:T(4,128)(2,1)S(1)} async-done(((bf16[4,200,2,4,128]{1,3,2,0,4:T(4,128)(2,1)}), bf16[4,200,2,4,128]{1,3,2,0,4:T(4,128)(2,1)S(1)}, u32[]{:S(2)}, u32[]{:S(2)}) %all-to-all-start) | async-done | bytes 1638432 | tf_op jit(solution)/shard_map/all_to_all | solution.py:38
  89.0 5.3 gather_fusion.1
  94.4 2.9 copy.119
  98.8 5.2 all_to_all.35
  106.0 13.1 %fusion.11 = f32[128,9,4,200,4]{3,1,4,2,0:T(8,128)} fusion(bf16[200,4,4,128,1]{0,2,1,4,3:T(4,128)(2,1)S(1)} %bitcast.135, bf16[1,1,9,4,4,128]{2,3,4,5,1,0:T(4,128)(2,1)} %copy.164), kind=kOutput, calls=%fused_computation.24 | convolution fusion | flops 29491200 | bytes 15601664 | tf_op jit(solution)/shard_map/svak,mack->msvck/dot_general | solution.py:62
  119.2 17.8 %fusion.3 = bf16[9,200,4,4,128]{1,0,2,3,4:T(8,128)(2,1)} fusion(f32[128,9,4,200,4]{3,1,4,2,0:T(8,128)} %fusion.11, pred[4]{0:T(512)(128)(4,1)S(1)} %get-tuple-element.30, bf16[200,2,4,128]{0,1,2,3:T(2,128)(2,1)S(1)} %copy-done.2, bf16[9,4,2,128,1]{0,1,2,3,4:T(4,128)(2,1)S(1)} %copy-done.7), kind=kOutput, calls=%fused_computation.9 | convolution fusion | flops 25804800 | bytes 22546436 | tf_op jit(solution)/shard_map/swck,mvwk->msvck/dot_general | solution.py:69
  137.0 24.3 %copy.124 = bf16[9,200,4,4,128]{4,3,2,1,0:T(4,128)(2,1)} copy(bf16[9,200,4,4,128]{1,0,2,3,4:T(8,128)(2,1)} %fusion.3) | data formatting | bytes 14745600 | tf_op jit(solution)/shard_map/convert_element_type | solution.py:73
  161.3 12.9 %squeeze_stack_reshape.12 = bf16[1800,2048]{1,0:T(8,128)(2,1)} reshape(bf16[9,200,4,4,128]{4,3,2,1,0:T(4,128)(2,1)} %copy.124) | data formatting | bytes 14745600 | tf_op jit(solution)/shard_map/squeeze;stack;reshape | solution.py:76
  174.1 17.8 %fusion.2 = bf16[9,200,4,4,128]{1,0,2,3,4:T(8,128)(2,1)} fusion(f32[128,9,4,200,4]{3,1,4,2,0:T(8,128)} %fusion.11, pred[4]{0:T(512)(128)(4,1)S(1)} %get-tuple-element.31, bf16[200,2,4,128]{0,1,2,3:T(2,128)(2,1)S(1)} %copy.167, bf16[9,4,2,128,1]{0,1,2,3,4:T(4,128)(2,1)S(1)} %copy-done.6), kind=kOutput, calls=%fused_computation.7 | convolution fusion | flops 25804800 | bytes 22546436 | tf_op jit(solution)/shard_map/swck,mvwk->msvck/dot_general | solution.py:69
  192.0 24.3 %copy.127 = bf16[9,200,4,4,128]{4,3,2,1,0:T(4,128)(2,1)} copy(bf16[9,200,4,4,128]{1,0,2,3,4:T(8,128)(2,1)} %fusion.2) | data formatting | bytes 14745600 | tf_op jit(solution)/shard_map/convert_element_type | solution.py:73
  216.3 12.9 %squeeze_stack_reshape.13 = bf16[1800,2048]{1,0:T(8,128)(2,1)} reshape(bf16[9,200,4,4,128]{4,3,2,1,0:T(4,128)(2,1)} %copy.127) | data formatting | bytes 14745600 | tf_op jit(solution)/shard_map/squeeze;stack;reshape | solution.py:77
  229.3 6.4 fusion.26
  235.7 5.3 multiply_bitcast_fusion.1
  240.9 5.1 copy.128
  247.0 12.2 %fusion.7 = f32[128,9,4,200,4]{3,1,4,2,0:T(8,128)} fusion(bf16[200,4,4,128,1]{0,2,1,4,3:T(4,128)(2,1)S(1)} %bitcast.136, bf16[1,1,9,4,4,128]{2,3,4,5,1,0:T(4,128)(2,1)S(1)} %copy-done.4), kind=kOutput, calls=%fused_computation.20 | convolution fusion | flops 29491200 | bytes 15601664 | tf_op jit(solution)/shard_map/svak,mack->msvck/dot_general | solution.py:62
  259.1 17.8 %fusion.1 = bf16[9,200,4,4,128]{1,0,2,3,4:T(8,128)(2,1)} fusion(f32[128,9,4,200,4]{3,1,4,2,0:T(8,128)} %fusion.7, pred[4]{0:T(512)(128)(4,1)S(1)} %get-tuple-element.30, bf16[200,2,4,128]{0,1,2,3:T(2,128)(2,1)S(1)} %copy.171, bf16[9,4,2,128,1]{0,1,2,3,4:T(4,128)(2,1)S(1)} %get-tuple-element.21), kind=kOutput, calls=%fused_computation.5 | convolution fusion | flops 25804800 | bytes 22546436 | tf_op jit(solution)/shard_map/swck,mvwk->msvck/dot_general | solution.py:69
  277.0 24.3 %copy.133 = bf16[9,200,4,4,128]{4,3,2,1,0:T(4,128)(2,1)} copy(bf16[9,200,4,4,128]{1,0,2,3,4:T(8,128)(2,1)} %fusion.1) | data formatting | bytes 14745600 | tf_op jit(solution)/shard_map/convert_element_type | solution.py:73
  301.3 12.9 %squeeze_stack_reshape.14 = bf16[1800,2048]{1,0:T(8,128)(2,1)} reshape(bf16[9,200,4,4,128]{4,3,2,1,0:T(4,128)(2,1)} %copy.133) | data formatting | bytes 14745600 | tf_op jit(solution)/shard_map/squeeze;stack;reshape | solution.py:76
  314.2 8.4 %fusion.27 = f32[1800,400]{0,1:T(8,128)} fusion(bf16[1800,2048]{1,0:T(8,128)(2,1)} %squeeze_stack_reshape.14, bf16[400,2048]{1,0:T(8,128)(2,1)S(1)} %copy-done.9), kind=kOutput, calls=%fused_computation.76 | convolution fusion | flops 2949120000 | bytes 11891200 | tf_op jit(solution)/shard_map/dot_general | solution.py:47
  322.6 18.1 %fusion = bf16[9,200,4,4,128]{1,0,2,3,4:T(8,128)(2,1)} fusion(f32[128,9,4,200,4]{3,1,4,2,0:T(8,128)} %fusion.7, pred[4]{0:T(512)(128)(4,1)S(1)} %get-tuple-element.31, bf16[200,2,4,128]{0,1,2,3:T(2,128)(2,1)S(1)} %copy-done.1, bf16[9,4,2,128,1]{0,1,2,3,4:T(4,128)(2,1)S(1)} %copy-done.5), kind=kOutput, calls=%fused_computation.3 | convolution fusion | flops 25804800 | bytes 22546436 | tf_op jit(solution)/shard_map/swck,mvwk->msvck/dot_general | solution.py:69
  340.7 24.3 %copy.136 = bf16[9,200,4,4,128]{4,3,2,1,0:T(4,128)(2,1)} copy(bf16[9,200,4,4,128]{1,0,2,3,4:T(8,128)(2,1)} %fusion) | data formatting | bytes 14745600 | tf_op jit(solution)/shard_map/convert_element_type | solution.py:73
  365.0 12.8 %squeeze_stack_reshape.15 = bf16[1800,2048]{1,0:T(8,128)(2,1)} reshape(bf16[9,200,4,4,128]{4,3,2,1,0:T(4,128)(2,1)} %copy.136) | data formatting | bytes 14745600 | tf_op jit(solution)/shard_map/squeeze;stack;reshape | solution.py:77
  377.9 8.1 %multiply_bitcast_fusion = f32[400,1800]{1,0:T(8,128)S(1)} fusion(f32[1800,400]{0,1:T(8,128)} %fusion.27, bf16[1800,2048]{1,0:T(8,128)(2,1)} %squeeze_stack_reshape.15, bf16[400,2048]{1,0:T(8,128)(2,1)} %reshape.78), kind=kOutput, calls=%fused_computation.10 | convolution fusion | flops 2950559744 | bytes 14771200 | tf_op jit(solution)/shard_map/dot_general | solution.py:47
  386.0 3.1 copy.137
  391.0 255.6 %all-reduce.5.cloned.1.call-done = (f32[400,9,200]{0,2,1:T(8,128)}, f32[400,9,200]{0,2,1:T(8,128)}) async-done(((f32[400,9,200]{0,2,1:T(8,128)}, f32[400,9,200]{0,2,1:T(8,128)}), (f32[400,9,200]{0,2,1:T(8,128)}, f32[400,9,200]{0,2,1:T(8,128)})) %all-reduce.5.cloned.1.call-update) | async-done | bytes 5760016
  (73 shorter events, 38.7 us)
Async XLA Ops:
  9.3 9.9 %copy-start.11 = (s32[4,512]{1,0:T(4,128)S(1)}, s32[4,512]{1,0:T(4,128)}, u32[]{:S(2)}) copy-start(s32[4,512]{1,0:T(4,128)} %param.9) | copy-start | bytes 24580
  9.3 22.4 %all-to-all-start.2 = ((bf16[4,200,2,4,128]{4,1,3,2,0:T(8,128)(2,1)}), bf16[4,200,2,4,128]{4,1,3,2,0:T(8,128)(2,1)}, u32[]{:S(2)}, u32[]{:S(2)}) async-start(bf16[4,200,2,4,128]{4,1,3,2,0:T(8,128)(2,1)} %copy.121), calls=%async_computation.2 | async-start | bytes 3276800 | tf_op jit(solution)/shard_map/all_to_all | solution.py:54
  28.3 10.6 %copy-start.10 = (bf16[2,4,9,4,4,128]{5,4,3,2,1,0:T(4,128)(2,1)S(1)}, bf16[2,4,9,4,4,128]{5,4,3,2,1,0:T(4,128)(2,1)}, u32[]{:S(2)}) copy-start(bf16[2,4,9,4,4,128]{5,4,3,2,1,0:T(4,128)(2,1)} %param.8) | copy-start | bytes 884740
  31.7 55.2 %all-to-all-start = ((bf16[4,200,2,4,128]{1,3,2,0,4:T(4,128)(2,1)}), bf16[4,200,2,4,128]{1,3,2,0,4:T(4,128)(2,1)S(1)}, u32[]{:S(2)}, u32[]{:S(2)}) async-start(bf16[4,200,2,4,128]{1,3,2,0,4:T(4,128)(2,1)} %fusion.4), calls=%async_computation | async-start | bytes 4194304 | tf_op jit(solution)/shard_map/all_to_all | solution.py:38
  38.0 31.8 %all-gather.2.cloned.1.call-start = ((), (), s32[]{:S(2)}) async-start(), calls=%async_computation.3 | async-start | bytes 2457600 | tf_op jit(solution)/shard_map/all_gather | solution.py:26
  38.8 607.8 %all-reduce.5.cloned.1.call-start = ((), (), s32[]{:S(2)}) async-start(), calls=%async_computation.4 | async-start | bytes 14745600
  106.0 13.1 %copy-start.2 = (bf16[200,2,4,128]{0,1,2,3:T(2,128)(2,1)S(1)}, bf16[200,2,4,128]{0,1,2,3:T(2,128)(2,1)}, u32[]{:S(2)}) copy-start(bf16[200,2,4,128]{0,1,2,3:T(2,128)(2,1)} %copy.166) | copy-start | bytes 1228804
  106.0 13.1 %copy-start.7 = (bf16[9,4,2,128,1]{0,1,2,3,4:T(4,128)(2,1)S(1)}, bf16[9,4,2,128,1]{0,1,2,3,4:T(4,128)(2,1)}, u32[]{:S(2)}) copy-start(bf16[9,4,2,128,1]{0,1,2,3,4:T(4,128)(2,1)} %get-tuple-element.19) | copy-start | bytes 55300
  161.3 12.9 %copy-start.6 = (bf16[9,4,2,128,1]{0,1,2,3,4:T(4,128)(2,1)S(1)}, bf16[9,4,2,128,1]{0,1,2,3,4:T(4,128)(2,1)}, u32[]{:S(2)}) copy-start(bf16[9,4,2,128,1]{0,1,2,3,4:T(4,128)(2,1)} %get-tuple-element.18) | copy-start | bytes 55300
  216.3 12.9 %copy-start.8 = (bf16[400,2048]{1,0:T(8,128)(2,1)S(1)}, bf16[400,2048]{1,0:T(8,128)(2,1)}, u32[]{:S(2)}) copy-start(bf16[400,2048]{1,0:T(8,128)(2,1)} %reshape.78) | copy-start | bytes 4915204
  229.3 6.4 copy-start
  240.9 5.1 copy-start.3
  240.9 6.0 copy-start.4
  301.3 12.9 %copy-start.9 = (bf16[400,2048]{1,0:T(8,128)(2,1)S(1)}, bf16[400,2048]{1,0:T(8,128)(2,1)}, u32[]{:S(2)}) copy-start(bf16[400,2048]{1,0:T(8,128)(2,1)} %reshape.78) | copy-start | bytes 4915204
  314.2 8.4 %copy-start.1 = (bf16[200,2,4,128]{0,1,2,3:T(2,128)(2,1)S(1)}, bf16[200,2,4,128]{0,1,2,3:T(2,128)(2,1)}, u32[]{:S(2)}) copy-start(bf16[200,2,4,128]{0,1,2,3:T(2,128)(2,1)} %copy.172) | copy-start | bytes 1228804
  314.2 8.4 %copy-start.5 = (bf16[9,4,2,128,1]{0,1,2,3,4:T(4,128)(2,1)S(1)}, bf16[9,4,2,128,1]{0,1,2,3,4:T(4,128)(2,1)}, u32[]{:S(2)}) copy-start(bf16[9,4,2,128,1]{0,1,2,3,4:T(4,128)(2,1)} %get-tuple-element.20) | copy-start | bytes 55300
  389.1 0.7 copy-start.12
Sparse Core Ops, SparseCore 0:
  40.4 29.4 all-gather.1
  389.2 257.2 all-reduce.4
where the time goes:
time: 670 us; the launch traced here: 660 us
  waiting for transfers between devices  282 us (42%)
  local copies, waits for them, and re-layouts  215 us (32%)
  matrix products  125 us (19%)
  between operations  14.7 us (2%)
  starting transfers between devices  11.1 us (2%)
  other arithmetic  7.46 us (1%)
    unnamed x3, waiting for transfers between devices  256 us
    convert_element_type x4, local copies, waits for them, and re-layouts, local(): table_h = (jnp.where(inside, elec, 0.0) - hole).astype(jnp.bfloat16)  97.3 us
    dot_general x4, matrix products, local(): jnp.einsum('swck,mvwk->msvck', coef_part, hole_table, preferred_element_t...  71.6 us
    dot_general x4, matrix products, contract(): lax.dot_general(rows, table, (((1,), (1,)), ((), ())), preferred_element_...  28.1 us
    another operation x2, local copies, waits for them, and re-layouts, local(): total = contract(stacked_tables[0], zero_flat)  25.8 us
    another operation x2, local copies, waits for them, and re-layouts, local(): total = total + contract(stacked_tables[1], zero_flat)  25.8 us
    dot_general x2, matrix products, local(): jnp.einsum('svak,mack->msvck', full_shifted[group], couple_q[0], preferre...  25.3 us
    unnamed x37, local copies, waits for them, and re-layouts  19.2 us
  transfers between devices with their start and end apart: 4, of which 3 were waited for; matrix products, arithmetic and copies ran while one was open for 6% of the time, Pallas kernels for 0%

commit v1 on v0

v1 whole, which is shorter than its diff:
```python
import functools

import jax
import jax.numpy as jnp
from jax import lax
from jax.experimental import pallas as pl
from jax.experimental.pallas import tpu as pltpu
from jax.sharding import PartitionSpec as P

PEERS = 4
ROWS = 16
LANES = 128
COLS = 384
LIMIT = 40 * 2**20


def round_up(n, unit):
    return (n + unit - 1) // unit * unit


def pick_kernel(x_ref, sel_ref, out_ref):
    nrow, width, _ = sel_ref.shape
    wide = sel_ref.shape[2]
    for d in range(nrow):
        for v in range(x_ref.shape[1] // width):
            got = jnp.dot(
                x_ref[:, v * width : (v + 1) * width], sel_ref[d], preferred_element_type=jnp.float32
            )
            out_ref[d, :, v * wide : (v + 1) * wide] = got.astype(jnp.bfloat16)


def build_table(x_ref, c_ref, table, modes, nval, ncond, elec):
    rows = x_ref.shape[0]

    def chunk(r, carry):
        at = pl.multiple_of(r * ROWS, ROWS)

        def slab(g):
            piece = x_ref[pl.ds(at, ROWS), g * LANES : (g + 1) * LANES]
            return piece.astype(jnp.float32).reshape(ROWS // 8, 8, LANES)

        for outer in range(nval if elec else ncond):
            if elec:
                slabs = [slab(outer * ncond + a) for a in range(ncond)]
            else:
                slabs = [slab(w * ncond + outer) for w in range(nval)]
            for m in range(modes):
                for inner in range(ncond if elec else nval):
                    if elec:
                        ids = [(m * ncond + a) * ncond + inner for a in range(ncond)]
                        g = outer * ncond + inner
                    else:
                        ids = [(m * nval + inner) * nval + w for w in range(nval)]
                        g = inner * ncond + outer
                    total = slabs[0] * c_ref[ids[0]][None]
                    for one, i in zip(slabs[1:], ids[1:]):
                        total = total + one * c_ref[i][None]
                    table[pl.ds(m * rows + at, ROWS), g * LANES : (g + 1) * LANES] = total.reshape(
                        ROWS, LANES
                    ).astype(jnp.bfloat16)
        return carry

    lax.fori_loop(0, rows // ROWS, chunk, 0)
    used = modes * rows
    if used < table.shape[0]:
        table[used:, :] = jnp.zeros((table.shape[0] - used, table.shape[1]), jnp.bfloat16)


def contract(z_ref, table, write):
    def cols(j, carry):
        at = pl.multiple_of(j * COLS, COLS)
        write(
            at,
            lax.dot_general(
                z_ref[...],
                table[pl.ds(at, COLS), :],
                (((1,), (1,)), ((), ())),
                preferred_element_type=jnp.float32,
            ),
        )
        return carry

    lax.fori_loop(0, table.shape[0] // COLS, cols, 0)


def hole_kernel(modes, nval, ncond, x_ref, c_ref, z_ref, out_ref, table):
    build_table(x_ref, c_ref, table, modes, nval, ncond, False)

    def write(at, got):
        out_ref[:, pl.ds(at, COLS)] = got

    contract(z_ref, table, write)


def elec_kernel(modes, nval, ncond, f_ref, inc_ref, perm_ref, c_ref, z_ref, hole_ref, out_ref, x_ref, table):
    nrow = inc_ref.shape[0]
    wide = inc_ref.shape[2] // nval
    width = perm_ref.shape[1]
    for v in range(nval):
        got = jnp.zeros((x_ref.shape[0], width), jnp.float32)
        for o in range(nrow):
            got = got + jnp.dot(
                inc_ref[o, :, v * wide : (v + 1) * wide],
                perm_ref[o * wide : (o + 1) * wide, :],
                preferred_element_type=jnp.float32,
            )
        x_ref[:, v * width : (v + 1) * width] = got.astype(jnp.bfloat16)
    build_table(x_ref, c_ref, table, modes, nval, ncond, True)
    factor = f_ref[0]

    def write(at, got):
        out_ref[:, pl.ds(at, COLS)] = (got - hole_ref[:, pl.ds(at, COLS)]) * factor

    contract(z_ref, table, write)


def local(coef_zero, coef_shift, coupling, partner):
    nrow = lax.axis_size("krow")
    me = lax.axis_index("krow")
    nband = lax.axis_size("band")
    half = lax.axis_index("band")
    nexc = lax.axis_size("exc")
    exc = lax.axis_index("exc")
    mine, nval, ncond, kdev = coef_zero.shape
    nq, share, lower = coef_shift.shape[:3]
    modes = coupling.shape[2]
    cap = kdev // PEERS
    pairs = nval * ncond
    depth = pairs * kdev
    groups = nq // nband
    states = mine * nexc
    kept = states // nrow
    kept_pad = round_up(kept, 8)
    rows = round_up(share, ROWS)
    cols = round_up(modes * rows, COLS)
    scale = (1.0 * pairs * nrow * kdev) ** (-0.5)

    flat = jnp.pad(coef_shift.reshape(nq, share, lower * ncond * kdev), ((0, 0), (0, rows - share), (0, 0)))
    keep = lax.dynamic_slice_in_dim(flat, half * groups, groups, axis=0)
    give = lax.dynamic_slice_in_dim(flat, (nband - 1 - half) * groups, groups, axis=0)
    got = lax.ppermute(give, "band", [(0, 1), (1, 0)])
    first = half == 0
    full = jnp.concatenate([jnp.where(first, keep, got), jnp.where(first, got, keep)], axis=2)

    part = lax.dynamic_slice_in_dim(partner, half * groups, groups, axis=0)
    owner = (part // kdev).reshape(groups, nrow, kdev)
    within = (part % kdev).reshape(groups, nrow, kdev)
    ids = jnp.arange(kdev, dtype=jnp.int32)
    slots = jnp.arange(cap, dtype=jnp.int32)
    tri = (ids[:, None] <= ids[None, :]).astype(jnp.bfloat16)
    eye = jnp.eye(ncond, dtype=jnp.bfloat16)

    def ranked(flags):
        counts = jnp.einsum("qdk,kl->qdl", flags.astype(jnp.bfloat16), tri, preferred_element_type=jnp.float32)
        return flags[..., None] & (counts.astype(jnp.int32)[..., None] - 1 == slots)

    chosen = ranked(owner == me).astype(jnp.bfloat16)
    places = (within[..., None] == ids).astype(jnp.bfloat16)
    select = jnp.einsum("qdkx,qdkj->qdxj", places, chosen, preferred_element_type=jnp.float32).astype(jnp.bfloat16)
    select = (eye[:, None, :, None] * select[:, :, None, :, None, :]).reshape(
        groups, nrow, ncond * kdev, ncond * cap
    )
    my_owner = lax.dynamic_index_in_dim(owner, me, axis=1, keepdims=False)
    match = my_owner[:, None, :] == jnp.arange(nrow, dtype=jnp.int32)[None, :, None]
    perm = jnp.swapaxes(ranked(match), 2, 3).astype(jnp.bfloat16)
    perm = (eye[:, None, :, None] * perm[:, :, None, :, None, :]).reshape(
        groups, nrow * ncond * cap, ncond * kdev
    )

    incoming = []
    for g in range(groups):
        outgoing = pl.pallas_call(
            pick_kernel,
            out_shape=jax.ShapeDtypeStruct((nrow, rows, pairs * cap), jnp.bfloat16),
            compiler_params=pltpu.CompilerParams(vmem_limit_bytes=LIMIT),
            name="pick",
        )(full[g], select[g])
        incoming.append(lax.all_to_all(outgoing, "krow", split_axis=0, concat_axis=0, tiled=True))

    zero = coef_zero.reshape(mine, depth)
    if nexc == 2:
        other = lax.ppermute(zero, "exc", [(0, 1), (1, 0)])
        lead = exc == 0
        whole = jnp.concatenate([jnp.where(lead, zero, other), jnp.where(lead, other, zero)], axis=0)
    else:
        whole = lax.all_gather(zero, "exc", axis=0, tiled=True)
    whole = jnp.pad(whole.reshape(nrow, kept, depth), ((0, 0), (0, kept_pad - kept), (0, 0)))
    whole = whole.reshape(nrow * kept_pad, depth)

    tops = jnp.stack([jnp.max(jnp.abs(a)).astype(jnp.float32) for a in (coef_zero, coef_shift, coupling)])
    tops = lax.pmax(tops, ("krow", "exc", "band"))
    bound = tops[0] * tops[1] * tops[2] * (2.0 * ncond * depth * nrow)
    factor = 32768.0 / jnp.maximum(bound, 1e-30)

    couple = lax.dynamic_slice_in_dim(coupling, half * groups, groups, axis=1).astype(jnp.float32)
    couple = couple.reshape(2, groups, modes * ncond * ncond, 1, kdev)
    couple = jnp.broadcast_to(couple, couple.shape[:3] + (8, kdev))

    macs = rows * modes * depth * 4 + whole.shape[0] * cols * depth
    cost = pl.CostEstimate(flops=8 * macs, bytes_accessed=8 * 2**20, transcendentals=0)
    smem = pl.BlockSpec(memory_space=pltpu.SMEM)
    vmem = pl.BlockSpec(memory_space=pltpu.VMEM)
    partial_shape = jax.ShapeDtypeStruct((nrow * kept_pad, cols), jnp.float32)
    table = pltpu.VMEM((cols, depth), jnp.bfloat16)
    params = pltpu.CompilerParams(vmem_limit_bytes=LIMIT)
    holes = [
        pl.pallas_call(
            functools.partial(hole_kernel, modes, nval, ncond),
            out_shape=partial_shape,
            scratch_shapes=[table],
            compiler_params=params,
            cost_estimate=cost,
            name="hole",
        )(full[g], couple[1, g], whole)
        for g in range(groups)
    ]

    pieces = []
    for g in range(groups):
        partial = pl.pallas_call(
            functools.partial(elec_kernel, modes, nval, ncond),
            out_shape=partial_shape,
            in_specs=[smem] + [vmem] * 5,
            out_specs=vmem,
            scratch_shapes=[pltpu.VMEM((rows, depth), jnp.bfloat16), table],
            compiler_params=params,
            cost_estimate=cost,
            name="elec",
        )(factor.reshape(1), incoming[g], perm[g], couple[0, g], whole, holes[g])
        blocks = partial.reshape(nrow, kept_pad, cols)

        def block(d):
            return lax.dynamic_index_in_dim(blocks, jnp.clip(d, 0, nrow - 1), axis=0, keepdims=False)

        up = down = None
        for t in range(1, nrow):
            send_up, send_down = block(me + nrow - t), block(me - nrow + t)
            if up is not None:
                send_up = send_up + up.astype(jnp.float32)
                send_down = send_down + down.astype(jnp.float32)
            up = lax.ppermute(send_up.astype(jnp.float16), "krow", [(z, z + 1) for z in range(t)])
            down = lax.ppermute(
                send_down.astype(jnp.float16), "krow", [(z, z - 1) for z in range(nrow - t, nrow)]
            )
        total = block(me)
        if up is not None:
            total = total + up.astype(jnp.float32) + down.astype(jnp.float32)
        total = total[:kept, : modes * rows].reshape(kept, modes, rows)[:, :, :share]
        pieces.append(total * (scale / factor))
    return jnp.stack(pieces, axis=1)


def solution(mesh):
    placed = (
        P(("grp", "exc"), None, None, "krow"),
        P(None, ("grp", "exc"), "band", None, "krow"),
        P(None, "grp", None, None, None, "krow"),
        P(),
    )
    return jax.shard_map(
        local,
        mesh=mesh,
        in_specs=placed,
        out_specs=P(("grp", "krow"), "band", None, "exc"),
        check_vma=False,
    )
```

time: 670 us -> 233 us (0.35); the launches traced: 660 us -> 230 us
  waiting for transfers between devices: 282 us -> 24.7 us
  local copies, waits for them, and re-layouts: 215 us -> 58.4 us
  matrix products: 125 us -> 0.6 us
  Pallas kernels: 0 us -> 44.9 us
  starting transfers between devices: 11.1 us -> 40 us
  blocking collectives: 5.21 us -> 33.2 us
  other arithmetic: 7.46 us -> 25.6 us
  between operations: 14.7 us -> 2.57 us
    unnamed x3 -> x0, waiting for transfers between devices: 256 us -> none
    dot_general x10 -> x3, matrix products: 125 us -> 0.6 us  [the longest x1 0.32 us: local(): jnp.einsum('qdkx,qdkj->qdxj', places, chosen, preferred_element_type=jnp....]
    convert_element_type x4 -> x1, local copies, waits for them, and re-layouts: 97.3 us -> 0.11 us  [local(): eye = jnp.eye(ncond, dtype=jnp.bfloat16)]
    another operation x7 -> x1, local copies, waits for them, and re-layouts: 57.5 us -> 2.34 us  [local(): return jnp.stack(pieces, axis=1)]
    pallas_call x0 -> x6, Pallas kernels: none -> 44.9 us  [the longest x2 22.1 us: local(): pl.pallas_call(functools.partial(elec_kernel, modes, nval, ncond), out_sh...]
    pmax x0 -> x1, blocking collectives: none -> 33.2 us  [local(): tops = lax.pmax(tops, ('krow', 'exc', 'band'))]
    ppermute x0 -> x14, starting transfers between devices: none -> 31.1 us  [the longest x6 21.1 us: local(): lax.ppermute(send_up.astype(jnp.float16), 'krow', [(z, z + 1) for z in ra...]
    ppermute x0 -> x14, waiting for transfers between devices: none -> 24.7 us  [the longest x6 24.6 us: local(): lax.ppermute(send_up.astype(jnp.float16), 'krow', [(z, z + 1) for z in ra...]
  transfers between devices with their start and end apart: 4 -> 16, of which waited for: 3 -> 5; matrix products, arithmetic and copies ran while one was open for 6% -> 27% of each run, Pallas kernels for 0% -> 14%
where the time goes in v1:
time: 233 us; the launch traced here: 230 us
  local copies, waits for them, and re-layouts  58.4 us (25%)
  Pallas kernels  44.9 us (19%)
  starting transfers between devices  40 us (17%)
  blocking collectives  33.2 us (14%)
  other arithmetic  25.6 us (11%)
  waiting for transfers between devices  24.7 us (11%)
  between operations  2.57 us (1%)
    pmax x1, blocking collectives, local(): tops = lax.pmax(tops, ('krow', 'exc', 'band'))  33.2 us
    ppermute x6, waiting for transfers between devices, local(): lax.ppermute(send_up.astype(jnp.float16), 'krow', [(z, z + 1) for z in ra...  24.6 us
    pallas_call x2, Pallas kernels, local(): pl.pallas_call(functools.partial(elec_kernel, modes, nval, ncond), out_sh...  22.1 us
    dynamic_slice x11, local copies, waits for them, and re-layouts, block(): lax.dynamic_index_in_dim(blocks, jnp.clip(d, 0, nrow - 1), axis=0, keepdi...  21.2 us
    ppermute x6, starting transfers between devices, local(): lax.ppermute(send_up.astype(jnp.float16), 'krow', [(z, z + 1) for z in ra...  21.1 us
    pallas_call x2, Pallas kernels, local(): pl.pallas_call(functools.partial(hole_kernel, modes, nval, ncond), out_sh...  18.9 us
    unnamed x62, local copies, waits for them, and re-layouts  18.7 us
    all_to_all x2, starting transfers between devices, local(): lax.all_to_all(outgoing, 'krow', split_axis=0, concat_axis=0, tiled=True)  8.82 us
  transfers between devices with their start and end apart: 16, of which 5 were waited for; matrix products, arithmetic and copies ran while one was open for 27% of the time, Pallas kernels for 14%

profile of v1, /device:TPU:0, one launch (start us, length us, event | category | flops | bytes accessed | tf_op | source)
XLA Modules:
  0.0 230.0 jit_solution(7249583573126224957)
XLA Ops:
  0.0 2.5 %reshape.87 = bf16[200,2048]{1,0:T(8,128)(2,1)} reshape(bf16[200,4,4,128]{3,2,1,0:T(4,128)(2,1)} %param.4) | data formatting | bytes 1638400 | tf_op jit(solution)/shard_map/reshape | solution.py:180
  2.5 2.9 %collective-permute-start.1 = (bf16[200,2048]{1,0:T(8,128)(2,1)}, bf16[200,2048]{1,0:T(8,128)(2,1)}, u32[]{:S(2)}, u32[]{:S(2)}) collective-permute-start(bf16[200,2048]{1,0:T(8,128)(2,1)} %reshape.87), channel_id=1, source_target_pairs={{0,2},{2,0},{1,3},{3,1},{4,6},{6,4},{5,7},{7,5},{8,10},{10,8},{9,1... | collective-permute-start | bytes 2457608 | tf_op jit(solution)/shard_map/ppermute | solution.py:182
  7.6 2.3 %abs_reduce_fusion = bf16[]{:T(256)} fusion(bf16[4,200,2,4,128]{4,3,2,1,0:T(4,128)(2,1)S(1)} %copy-done.12), kind=kLoop, calls=%fused_computation.4 | loop fusion | flops 1638399 | bytes 1638402 | tf_op jit(solution)/shard_map/reduce_max | solution.py:190
  13.6 2.0 maximum_convert_fusion
  15.5 33.2 %pmax.7 = f32[3]{0:T(128)S(1)} all-reduce(f32[3]{0:T(128)S(1)} %maximum_convert_fusion), channel_id=1, replica_groups=mesh['grp'=2,'krow'=4,'exc'=2,'band'=2] {'krow','exc','band'}, use_global_device_ids=true, to_apply=%region_3.4 | all-reduce | flops 3 | bytes 24 | tf_op jit(solution)/shard_map/pmax | solution.py:191
  61.1 2.7 %broadcast_select_fusion.3 = (bf16[200,2048]{1,0:T(8,128)(2,1)}, bf16[200,2048]{1,0:T(8,128)(2,1)}) fusion(bf16[200,2048]{1,0:T(8,128)(2,1)} %reshape.87, bf16[200,2048]{1,0:T(8,128)(2,1)} %collective-permute-done.1, pred[]{:T(512)S(6)} %eq.110), kind=kLoop, calls=%fused_computation.44 | loop fusion | flops 819200 | bytes 3276801 | tf_op jit(solution)/shard_map/jit(_where)/select_n | solution.py:184
  67.4 3.7 %all-to-all-start.1 = ((bf16[4,208,512]{2,1,0:T(8,128)(2,1)}), bf16[4,208,512]{2,1,0:T(8,128)(2,1)S(1)}, u32[]{:S(2)}, u32[]{:S(2)}) async-start(bf16[4,208,512]{2,1,0:T(8,128)(2,1)} %pick.3), calls=%async_computation.1 | async-start | bytes 1703936 | tf_op jit(solution)/shard_map/all_to_all | solution.py:178
  71.1 2.8 %pad_maximum_fusion.1 = bf16[400,2048]{1,0:T(8,128)(2,1)} fusion(bf16[200,2048]{1,0:T(8,128)(2,1)} %get-tuple-element.24, bf16[200,2048]{1,0:T(8,128)(2,1)} %get-tuple-element.23), kind=kLoop, calls=%fused_computation.3 | loop fusion | flops 3276800 | bytes 3276800 | tf_op jit(solution)/shard_map/concatenate | solution.py:184
  73.9 2.5 %reshape.88 = bf16[4,100,2048]{2,1,0:T(8,128)(2,1)} reshape(bf16[400,2048]{1,0:T(8,128)(2,1)} %pad_maximum_fusion.1) | data formatting | bytes 3276800 | tf_op jit(solution)/shard_map/reshape | solution.py:187
  80.0 9.4 %hole.3.hole_ref = f32[416,1920]{1,0:T(8,128)S(1)} custom-call(bf16[208,2048]{1,0:T(8,128)(2,1)S(1)} %get-tuple-element.22.x_ref, f32[144,8,128]{2,1,0:T(8,128)S(1)} %broadcast_in_dim.46.c_ref, bf16[416,2048]{1,0:T(8,128)(2,1)S(1)} %bitcast.93), custom_call_target="tpu_custom_call" | custom-call | flops 13208911872 | bytes 8388608 | tf_op jit(solution)/shard_map/hole/pallas_call | solution.py:207
  91.1 5.1 %all-to-all-start = ((bf16[4,208,512]{2,1,0:T(8,128)(2,1)}), bf16[4,208,512]{2,1,0:T(8,128)(2,1)}, u32[]{:S(2)}, u32[]{:S(2)}) async-start(bf16[4,208,512]{2,1,0:T(8,128)(2,1)} %pick.2), calls=%async_computation | async-start | bytes 1703936 | tf_op jit(solution)/shard_map/all_to_all | solution.py:178
  97.2 9.4 %hole.2.hole_ref = f32[416,1920]{1,0:T(8,128)S(1)} custom-call(bf16[208,2048]{1,0:T(8,128)(2,1)S(1)} %get-tuple-element.21.x_ref, f32[144,8,128]{2,1,0:T(8,128)S(1)} %broadcast_in_dim.42.c_ref, bf16[416,2048]{1,0:T(8,128)(2,1)S(1)} %bitcast.94), custom_call_target="tpu_custom_call" | custom-call | flops 13208911872 | bytes 8388608 | tf_op jit(solution)/shard_map/hole/pallas_call | solution.py:207
  109.6 10.5 %elec.3 = f32[416,1920]{1,0:T(8,128)S(1)} custom-call(f32[1]{0:T(128)S(6)} %div.25.f_ref, bf16[4,208,512]{2,1,0:T(8,128)(2,1)S(1)} %copy-done.5, bf16[512,512]{1,0:T(8,128)(2,1)S(1)} %bitcast.98, f32[144,8,128]{2,1,0:T(8,128)S(1)} %broadcast_in_dim.44.c_ref, bf16[416,2048]{1,0:T(8,128)(2,1)S(1)} %bitcast.95, f32[416,1920]{1,0:T(8,128)S(1)} %copy-done.9), custom_call_target="tpu_custom_call" | custom-call | flops 13208911872 | bytes 8388608 | tf_op jit(solution)/shard_map/elec/pallas_call | solution.py:220
  124.5 11.6 %elec.2 = f32[416,1920]{1,0:T(8,128)S(1)} custom-call(f32[1]{0:T(128)S(6)} %div.25.f_ref, bf16[4,208,512]{2,1,0:T(8,128)(2,1)} %all-to-all-done.inc_ref, bf16[512,512]{1,0:T(8,128)(2,1)S(1)} %bitcast.97, f32[144,8,128]{2,1,0:T(8,128)S(1)} %broadcast_in_dim.40.c_ref, bf16[416,2048]{1,0:T(8,128)(2,1)S(1)} %bitcast.96, f32[416,1920]{1,0:T(8,128)S(1)} %copy-done.11), custom_call_target="tpu_custom_call" | custom-call | flops 13208911872 | bytes 8388608 | tf_op jit(solution)/shard_map/elec/pallas_call | solution.py:220
  136.2 4.2 %constant_dynamic-slice_fusion.3 = (f32[1,104,1920]{2,1,0:T(8,128)}, f32[1,104,1920]{2,1,0:T(8,128)}, f32[1,104,1920]{2,1,0:T(8,128)}, f32[1,104,1920]{2,1,0:T(8...) fusion(f32[4,104,1920]{2,1,0:T(8,128)S(1)} %bitcast.91, ...), kind=kLoop, calls=%fused_computation.77 | loop fusion | bytes 22364188 | tf_op jit(solution)/shard_map/jit(dynamic_index_in_dim)/dynamic_slice | solution.py:233
  142.1 4.9 %collective-permute-start.8 = (f16[104,1920]{0,1:T(8,128)(2,1)S(1)}, f16[104,1920]{0,1:T(8,128)(2,1)}, u32[]{:S(2)}, u32[]{:S(2)}) collective-permute-start(f16[104,1920]{0,1:T(8,128)(2,1)S(1)} %convert_bitcast_fusion.1), channel_id=1, source_target_pairs={{0,4},{1,5},{2,6},{3,7},{16,20},{17,21},{18,22},{19,23}} | collective-permute-start | bytes 1198088 | tf_op jit(solution)/shard_map/ppermute | solution.py:241
  155.3 2.4 %copy.17 = f32[1,104,1920]{1,2,0:T(8,128)} copy(f32[1,104,1920]{2,1,0:T(8,128)} %get-tuple-element.18) | data formatting | bytes 1597440 | tf_op jit(solution)/shard_map/jit(dynamic_index_in_dim)/dynamic_slice | solution.py:233
  160.5 2.4 %copy.11 = f32[1,104,1920]{1,2,0:T(8,128)} copy(f32[1,104,1920]{2,1,0:T(8,128)} %get-tuple-element.40) | data formatting | bytes 1597440 | tf_op jit(solution)/shard_map/jit(dynamic_index_in_dim)/dynamic_slice | solution.py:233
  162.9 2.4 %copy.26 = f32[1,104,1920]{1,2,0:T(8,128)} copy(f32[1,104,1920]{2,1,0:T(8,128)} %get-tuple-element.41) | data formatting | bytes 1597440
  165.3 2.1 convert_bitcast_fusion.2
  168.9 2.4 %copy.13 = f32[1,104,1920]{1,2,0:T(8,128)} copy(f32[1,104,1920]{2,1,0:T(8,128)} %get-tuple-element.42) | data formatting | bytes 1597440 | tf_op jit(solution)/shard_map/jit(dynamic_index_in_dim)/dynamic_slice | solution.py:233
  171.3 2.4 %copy.14 = f32[1,104,1920]{1,2,0:T(8,128)} copy(f32[1,104,1920]{2,1,0:T(8,128)} %get-tuple-element.43) | data formatting | bytes 1597440 | tf_op jit(solution)/shard_map/jit(dynamic_index_in_dim)/dynamic_slice | solution.py:233
  173.8 2.5 %copy.25 = f32[1,104,1920]{1,2,0:T(8,128)} copy(f32[1,104,1920]{2,1,0:T(8,128)} %get-tuple-element.44) | data formatting | bytes 1597440
  185.6 5.2 %collective-permute-done.2 = f16[104,1920]{0,1:T(8,128)(2,1)S(1)} collective-permute-done((f16[104,1920]{0,1:T(8,128)(2,1)S(1)}, f16[104,1920]{0,1:T(8,128)(2,1)S(1)}, u32[]{:S(2)}, u32[]{:S(2)}) %collective-permute-start.2) | collective-permute-done | bytes 399392 | tf_op jit(solution)/shard_map/ppermute | solution.py:241
  190.9 4.5 %collective-permute-start.3 = (f16[104,1920]{0,1:T(8,128)(2,1)S(1)}, f16[104,1920]{0,1:T(8,128)(2,1)S(1)}, u32[]{:S(2)}, u32[]{:S(2)}) collective-permute-start(f16[104,1920]{0,1:T(8,128)(2,1)S(1)} %fusion.8), channel_id=1, source_target_pairs={{0,4},{4,8},{1,5},{5,9},{2,6},{6,10},{3,7},{7,11},{16,20},{20,24},... | collective-permute-start | bytes 1198088 | tf_op jit(solution)/shard_map/ppermute | solution.py:241
  196.9 4.4 %collective-permute-done.9 = f16[104,1920]{0,1:T(8,128)(2,1)S(1)} collective-permute-done((f16[104,1920]{0,1:T(8,128)(2,1)S(1)}, f16[104,1920]{0,1:T(8,128)(2,1)S(1)}, u32[]{:S(2)}, u32[]{:S(2)}) %collective-permute-start.9) | collective-permute-done | bytes 399392 | tf_op jit(solution)/shard_map/ppermute | solution.py:241
  201.4 4.5 %collective-permute-start.10 = (f16[104,1920]{0,1:T(8,128)(2,1)S(1)}, f16[104,1920]{0,1:T(8,128)(2,1)S(1)}, u32[]{:S(2)}, u32[]{:S(2)}) collective-permute-start(f16[104,1920]{0,1:T(8,128)(2,1)S(1)} %fusion.5), channel_id=1, source_target_pairs={{0,4},{4,8},{8,12},{1,5},{5,9},{9,13},{2,6},{6,10},{10,14},{3,7},{... | collective-permute-start | bytes 1198088 | tf_op jit(solution)/shard_map/ppermute | solution.py:241
  207.5 4.4 %collective-permute-done.3 = f16[104,1920]{0,1:T(8,128)(2,1)S(1)} collective-permute-done((f16[104,1920]{0,1:T(8,128)(2,1)S(1)}, f16[104,1920]{0,1:T(8,128)(2,1)S(1)}, u32[]{:S(2)}, u32[]{:S(2)}) %collective-permute-start.3) | collective-permute-done | bytes 399392 | tf_op jit(solution)/shard_map/ppermute | solution.py:241
  212.0 4.4 %collective-permute-start.4 = (f16[104,1920]{0,1:T(8,128)(2,1)S(1)}, f16[104,1920]{0,1:T(8,128)(2,1)S(1)}, u32[]{:S(2)}, u32[]{:S(2)}) collective-permute-start(f16[104,1920]{0,1:T(8,128)(2,1)S(1)} %fusion.9), channel_id=1, source_target_pairs={{0,4},{4,8},{8,12},{1,5},{5,9},{9,13},{2,6},{6,10},{10,14},{3,7},{... | collective-permute-start | bytes 1198088 | tf_op jit(solution)/shard_map/ppermute | solution.py:241
  216.4 5.6 %collective-permute-done.10 = f16[104,1920]{0,1:T(8,128)(2,1)S(1)} collective-permute-done((f16[104,1920]{0,1:T(8,128)(2,1)S(1)}, f16[104,1920]{0,1:T(8,128)(2,1)S(1)}, u32[]{:S(2)}, u32[]{:S(2)}) %collective-permute-start.10) | collective-permute-done | bytes 399392 | tf_op jit(solution)/shard_map/ppermute | solution.py:241
  222.3 5.0 %collective-permute-done.4 = f16[104,1920]{0,1:T(8,128)(2,1)S(1)} collective-permute-done((f16[104,1920]{0,1:T(8,128)(2,1)S(1)}, f16[104,1920]{0,1:T(8,128)(2,1)S(1)}, u32[]{:S(2)}, u32[]{:S(2)}) %collective-permute-start.4) | collective-permute-done | bytes 399392 | tf_op jit(solution)/shard_map/ppermute | solution.py:241
  227.6 2.3 %copy.24 = f32[100,2,9,200]{3,1,2,0:T(2,128)} copy(f32[100,2,9,200]{0,3,2,1:T(8,128)S(1)} %pad_maximum_fusion) | data formatting | bytes 2880000 | tf_op jit(solution)/shard_map/stack | solution.py:250
  (139 shorter events, 60.3 us)
Async XLA Ops:
  0.0 5.5 %copy-start.12 = (bf16[4,200,2,4,128]{4,3,2,1,0:T(4,128)(2,1)S(1)}, bf16[4,200,2,4,128]{4,3,2,1,0:T(4,128)(2,1)}, u32[]{:S(2)}) copy-start(bf16[4,200,2,4,128]{4,3,2,1,0:T(4,128)(2,1)} %param.5) | copy-start | bytes 4915204
  2.5 58.5 %collective-permute-start.1 = (bf16[200,2048]{1,0:T(8,128)(2,1)}, bf16[200,2048]{1,0:T(8,128)(2,1)}, u32[]{:S(2)}, u32[]{:S(2)}) collective-permute-start(bf16[200,2048]{1,0:T(8,128)(2,1)} %reshape.87), channel_id=1, source_target_pairs={{0,2},{2,0},{1,3},{3,1},{4,6},{6,4},{5,7},{7,5},{8,10},{10,8},{9,1... | collective-permute-start | bytes 2457608 | tf_op jit(solution)/shard_map/ppermute | solution.py:182
  7.6 3.9 %copy-start.27 = (s32[4,512]{1,0:T(4,128)S(1)}, s32[4,512]{1,0:T(4,128)}, u32[]{:S(2)}) copy-start(s32[4,512]{1,0:T(4,128)} %param.7) | copy-start | bytes 24580
  7.6 56.2 %collective-permute-start = (bf16[2,208,1024]{2,1,0:T(8,128)(2,1)}, bf16[2,208,1024]{2,1,0:T(8,128)(2,1)}, u32[]{:S(2)}, u32[]{:S(2)}) collective-permute-start(bf16[2,208,1024]{2,1,0:T(8,128)(2,1)} %pad_dynamic-slice_fusion), channel_id=1, source_target_pairs={{0,1},{1,0},{2,3},{3,2},{4,5},{5,4},{6,7},{7,6},{8,9},{9,8},{10,11... | collective-permute-start | bytes 2555912 | tf_op jit(solution)/shard_map/ppermute | solution.py:141
  67.4 23.7 %all-to-all-start.1 = ((bf16[4,208,512]{2,1,0:T(8,128)(2,1)}), bf16[4,208,512]{2,1,0:T(8,128)(2,1)S(1)}, u32[]{:S(2)}, u32[]{:S(2)}) async-start(bf16[4,208,512]{2,1,0:T(8,128)(2,1)} %pick.3), calls=%async_computation.1 | async-start | bytes 1703936 | tf_op jit(solution)/shard_map/all_to_all | solution.py:178
  91.1 6.1 %copy-start.1 = (bf16[4,104,2048]{2,1,0:T(8,128)(2,1)S(1)}, bf16[4,104,2048]{2,1,0:T(8,128)(2,1)}, u32[]{:S(2)}) copy-start(bf16[4,104,2048]{2,1,0:T(8,128)(2,1)} %copy-done) | copy-start | bytes 5111812
  91.1 15.6 %copy-start.4 = (bf16[4,208,512]{2,1,0:T(8,128)(2,1)}, bf16[4,208,512]{2,1,0:T(8,128)(2,1)S(1)}, u32[]{:S(2)}) copy-start(bf16[4,208,512]{2,1,0:T(8,128)(2,1)S(1)} %all-to-all-done.1.inc_ref) | copy-start | bytes 2555908
  91.1 29.0 %all-to-all-start = ((bf16[4,208,512]{2,1,0:T(8,128)(2,1)}), bf16[4,208,512]{2,1,0:T(8,128)(2,1)}, u32[]{:S(2)}, u32[]{:S(2)}) async-start(bf16[4,208,512]{2,1,0:T(8,128)(2,1)} %pick.2), calls=%async_computation | async-start | bytes 1703936 | tf_op jit(solution)/shard_map/all_to_all | solution.py:178
  97.2 11.2 %copy-start.2 = (bf16[4,104,2048]{2,1,0:T(8,128)(2,1)S(1)}, bf16[4,104,2048]{2,1,0:T(8,128)(2,1)}, u32[]{:S(2)}) copy-start(bf16[4,104,2048]{2,1,0:T(8,128)(2,1)} %copy-done) | copy-start | bytes 5111812
  97.2 11.2 %copy-start.7 = (bf16[64,8,4,128]{3,1,2,0:T(8,128)(2,1)S(1)}, bf16[64,8,4,128]{3,1,2,0:T(8,128)(2,1)}, u32[]{:S(2)}) copy-start(bf16[64,8,4,128]{3,1,2,0:T(8,128)(2,1)} %copy.33) | copy-start | bytes 1572868
  97.2 11.2 %copy-start.9 = (f32[416,1920]{1,0:T(8,128)S(1)}, f32[416,1920]{1,0:T(8,128)}, u32[]{:S(2)}) copy-start(f32[416,1920]{1,0:T(8,128)} %copy-done.8) | copy-start | bytes 9584644
  140.4 6.5 %copy-start.24 = (f32[1,104,1920]{2,1,0:T(8,128)S(1)}, f32[1,104,1920]{2,1,0:T(8,128)}, u32[]{:S(2)}) copy-start(f32[1,104,1920]{2,1,0:T(8,128)} %get-tuple-element.13) | copy-start | bytes 2396164
  142.0 6.3 %copy-start.23 = (f32[1,104,1920]{2,1,0:T(8,128)S(1)}, f32[1,104,1920]{2,1,0:T(8,128)}, u32[]{:S(2)}) copy-start(f32[1,104,1920]{2,1,0:T(8,128)} %get-tuple-element.14) | copy-start | bytes 2396164
  142.1 39.1 %collective-permute-start.8 = (f16[104,1920]{0,1:T(8,128)(2,1)S(1)}, f16[104,1920]{0,1:T(8,128)(2,1)}, u32[]{:S(2)}, u32[]{:S(2)}) collective-permute-start(f16[104,1920]{0,1:T(8,128)(2,1)S(1)} %convert_bitcast_fusion.1), channel_id=1, source_target_pairs={{0,4},{1,5},{2,6},{3,7},{16,20},{17,21},{18,22},{19,23}} | collective-permute-start | bytes 1198088 | tf_op jit(solution)/shard_map/ppermute | solution.py:241
  151.0 28.2 %collective-permute-start.11 = (f16[104,1920]{0,1:T(8,128)(2,1)}, f16[104,1920]{0,1:T(8,128)(2,1)}, u32[]{:S(2)}, u32[]{:S(2)}) collective-permute-start(f16[104,1920]{0,1:T(8,128)(2,1)} %convert_bitcast_fusion), channel_id=1, source_target_pairs={{12,8},{13,9},{14,10},{15,11},{28,24},{29,25},{30,26},{31,27}} | collective-permute-start | bytes 1198088 | tf_op jit(solution)/shard_map/ppermute | solution.py:242
  153.8 4.0 %copy-start.21 = (f32[1,104,1920]{2,1,0:T(8,128)S(1)}, f32[1,104,1920]{2,1,0:T(8,128)}, u32[]{:S(2)}) copy-start(f32[1,104,1920]{2,1,0:T(8,128)} %get-tuple-element.38) | copy-start | bytes 2396164
  167.4 16.3 %collective-permute-start.5 = (f16[104,1920]{0,1:T(8,128)(2,1)}, f16[104,1920]{0,1:T(8,128)(2,1)}, u32[]{:S(2)}, u32[]{:S(2)}) collective-permute-start(f16[104,1920]{0,1:T(8,128)(2,1)} %convert_bitcast_fusion.2), channel_id=1, source_target_pairs={{12,8},{13,9},{14,10},{15,11},{28,24},{29,25},{30,26},{31,27}} | collective-permute-start | bytes 1198088 | tf_op jit(solution)/shard_map/ppermute | solution.py:242
  176.3 4.9 %copy-start.16 = (f32[1,104,1920]{1,2,0:T(8,128)S(1)}, f32[1,104,1920]{1,2,0:T(8,128)}, u32[]{:S(2)}) copy-start(f32[1,104,1920]{1,2,0:T(8,128)} %copy.19) | copy-start | bytes 2396164
  177.7 6.0 %copy-start.17 = (f32[1,104,1920]{1,2,0:T(8,128)S(1)}, f32[1,104,1920]{1,2,0:T(8,128)}, u32[]{:S(2)}) copy-start(f32[1,104,1920]{1,2,0:T(8,128)} %copy.14) | copy-start | bytes 2396164
  177.7 13.1 %collective-permute-start.2 = (f16[104,1920]{0,1:T(8,128)(2,1)S(1)}, f16[104,1920]{0,1:T(8,128)(2,1)S(1)}, u32[]{:S(2)}, u32[]{:S(2)}) collective-permute-start(f16[104,1920]{0,1:T(8,128)(2,1)S(1)} %convert_bitcast_fusion.3), channel_id=1, source_target_pairs={{0,4},{1,5},{2,6},{3,7},{16,20},{17,21},{18,22},{19,23}} | collective-permute-start | bytes 1198088 | tf_op jit(solution)/shard_map/ppermute | solution.py:241
  180.3 10.4 %copy-start.14 = (f32[1,104,1920]{1,2,0:T(8,128)S(1)}, f32[1,104,1920]{1,2,0:T(8,128)}, u32[]{:S(2)}) copy-start(f32[1,104,1920]{1,2,0:T(8,128)} %copy.11) | copy-start | bytes 2396164
  180.3 15.1 %collective-permute-start.12 = (f16[104,1920]{0,1:T(8,128)(2,1)S(1)}, f16[104,1920]{0,1:T(8,128)(2,1)S(1)}, u32[]{:S(2)}, u32[]{:S(2)}) collective-permute-start(f16[104,1920]{0,1:T(8,128)(2,1)S(1)} %fusion.2), channel_id=1, source_target_pairs={{8,4},{12,8},{9,5},{13,9},{10,6},{14,10},{11,7},{15,11},{24,20},{2... | collective-permute-start | bytes 1198088 | tf_op jit(solution)/shard_map/ppermute | solution.py:242
  182.4 18.9 %collective-permute-start.9 = (f16[104,1920]{0,1:T(8,128)(2,1)S(1)}, f16[104,1920]{0,1:T(8,128)(2,1)S(1)}, u32[]{:S(2)}, u32[]{:S(2)}) collective-permute-start(f16[104,1920]{0,1:T(8,128)(2,1)S(1)} %fusion.4), channel_id=1, source_target_pairs={{0,4},{4,8},{1,5},{5,9},{2,6},{6,10},{3,7},{7,11},{16,20},{20,24},... | collective-permute-start | bytes 1198088 | tf_op jit(solution)/shard_map/ppermute | solution.py:241
  184.9 21.1 %collective-permute-start.6 = (f16[104,1920]{0,1:T(8,128)(2,1)S(1)}, f16[104,1920]{0,1:T(8,128)(2,1)S(1)}, u32[]{:S(2)}, u32[]{:S(2)}) collective-permute-start(f16[104,1920]{0,1:T(8,128)(2,1)S(1)} %fusion.6), channel_id=1, source_target_pairs={{8,4},{12,8},{9,5},{13,9},{10,6},{14,10},{11,7},{15,11},{24,20},{2... | collective-permute-start | bytes 1198088 | tf_op jit(solution)/shard_map/ppermute | solution.py:242
  190.9 15.1 %copy-start.13 = (f32[1,104,1920]{1,2,0:T(8,128)S(1)}, f32[1,104,1920]{1,2,0:T(8,128)}, u32[]{:S(2)}) copy-start(f32[1,104,1920]{1,2,0:T(8,128)} %copy.13) | copy-start | bytes 2396164
  190.9 20.9 %collective-permute-start.3 = (f16[104,1920]{0,1:T(8,128)(2,1)S(1)}, f16[104,1920]{0,1:T(8,128)(2,1)S(1)}, u32[]{:S(2)}, u32[]{:S(2)}) collective-permute-start(f16[104,1920]{0,1:T(8,128)(2,1)S(1)} %fusion.8), channel_id=1, source_target_pairs={{0,4},{4,8},{1,5},{5,9},{2,6},{6,10},{3,7},{7,11},{16,20},{20,24},... | collective-permute-start | bytes 1198088 | tf_op jit(solution)/shard_map/ppermute | solution.py:241
  195.6 20.8 %collective-permute-start.13 = (f16[104,1920]{0,1:T(8,128)(2,1)S(1)}, f16[104,1920]{0,1:T(8,128)(2,1)S(1)}, u32[]{:S(2)}, u32[]{:S(2)}) collective-permute-start(f16[104,1920]{0,1:T(8,128)(2,1)S(1)} %fusion.3), channel_id=1, source_target_pairs={{4,0},{8,4},{12,8},{5,1},{9,5},{13,9},{6,2},{10,6},{14,10},{7,3},{... | collective-permute-start | bytes 1198088 | tf_op jit(solution)/shard_map/ppermute | solution.py:242
  201.4 20.6 %copy-start.19 = (f32[1,104,1920]{1,2,0:T(8,128)S(1)}, f32[1,104,1920]{1,2,0:T(8,128)}, u32[]{:S(2)}) copy-start(f32[1,104,1920]{1,2,0:T(8,128)} %copy.17) | copy-start | bytes 2396164
  201.4 20.6 %collective-permute-start.10 = (f16[104,1920]{0,1:T(8,128)(2,1)S(1)}, f16[104,1920]{0,1:T(8,128)(2,1)S(1)}, u32[]{:S(2)}, u32[]{:S(2)}) collective-permute-start(f16[104,1920]{0,1:T(8,128)(2,1)S(1)} %fusion.5), channel_id=1, source_target_pairs={{0,4},{4,8},{8,12},{1,5},{5,9},{9,13},{2,6},{6,10},{10,14},{3,7},{... | collective-permute-start | bytes 1198088 | tf_op jit(solution)/shard_map/ppermute | solution.py:241
  206.2 16.1 %collective-permute-start.7 = (f16[104,1920]{0,1:T(8,128)(2,1)S(1)}, f16[104,1920]{0,1:T(8,128)(2,1)S(1)}, u32[]{:S(2)}, u32[]{:S(2)}) collective-permute-start(f16[104,1920]{0,1:T(8,128)(2,1)S(1)} %fusion.7), channel_id=1, source_target_pairs={{4,0},{8,4},{12,8},{5,1},{9,5},{13,9},{6,2},{10,6},{14,10},{7,3},{... | collective-permute-start | bytes 1198088 | tf_op jit(solution)/shard_map/ppermute | solution.py:242
  212.0 15.3 %collective-permute-start.4 = (f16[104,1920]{0,1:T(8,128)(2,1)S(1)}, f16[104,1920]{0,1:T(8,128)(2,1)S(1)}, u32[]{:S(2)}, u32[]{:S(2)}) collective-permute-start(f16[104,1920]{0,1:T(8,128)(2,1)S(1)} %fusion.9), channel_id=1, source_target_pairs={{0,4},{4,8},{8,12},{1,5},{5,9},{9,13},{2,6},{6,10},{10,14},{3,7},{... | collective-permute-start | bytes 1198088 | tf_op jit(solution)/shard_map/ppermute | solution.py:241
  222.0 5.3 %copy-start.18 = (f32[1,104,1920]{1,2,0:T(8,128)S(1)}, f32[1,104,1920]{1,2,0:T(8,128)}, u32[]{:S(2)}) copy-start(f32[1,104,1920]{1,2,0:T(8,128)} %copy.9) | copy-start | bytes 2396164
  (12 other events, 24.0 us)

commit v2 on v1

--- a/solution.py
+++ b/solution.py
@@ -29,32 +29,34 @@
             out_ref[d, :, v * wide : (v + 1) * wide] = got.astype(jnp.bfloat16)
 
 
-def build_table(x_ref, c_ref, table, modes, nval, ncond, elec):
-    rows = x_ref.shape[0]
+def build_table(x_ref, c_ref, y_ref, d_ref, table, modes, nval, ncond, lower):
+    rows = y_ref.shape[0]
 
     def chunk(r, carry):
         at = pl.multiple_of(r * ROWS, ROWS)
 
-        def slab(g):
-            piece = x_ref[pl.ds(at, ROWS), g * LANES : (g + 1) * LANES]
+        def slab(ref, g):
+            piece = ref[pl.ds(at, ROWS), g * LANES : (g + 1) * LANES]
             return piece.astype(jnp.float32).reshape(ROWS // 8, 8, LANES)
 
-        for outer in range(nval if elec else ncond):
-            if elec:
-                slabs = [slab(outer * ncond + a) for a in range(ncond)]
-            else:
-                slabs = [slab(w * ncond + outer) for w in range(nval)]
-            for m in range(modes):
-                for inner in range(ncond if elec else nval):
-                    if elec:
-                        ids = [(m * ncond + a) * ncond + inner for a in range(ncond)]
-                        g = outer * ncond + inner
-                    else:
-                        ids = [(m * nval + inner) * nval + w for w in range(nval)]
-                        g = inner * ncond + outer
-                    total = slabs[0] * c_ref[ids[0]][None]
-                    for one, i in zip(slabs[1:], ids[1:]):
-                        total = total + one * c_ref[i][None]
+        for v in range(nval):
+            own = [w for w in range(nval) if (w // lower == v // lower) == (x_ref is not None)]
+            if x_ref is not None:
+                shifted = [slab(x_ref, v * ncond + a) for a in range(ncond)]
+            for c in range(ncond):
+                held = [slab(y_ref, w * ncond + c) for w in own]
+                for m in range(modes):
+                    total = None
+                    for w, one in zip(own, held):
+                        term = one * d_ref[(m * nval + v) * nval + w][None]
+                        total = term if total is None else total + term
+                    if x_ref is not None:
+                        elec = None
+                        for a in range(ncond):
+                            term = shifted[a] * c_ref[(m * ncond + a) * ncond + c][None]
+                            elec = term if elec is None else elec + term
+                        total = elec - total
+                    g = v * ncond + c
                     table[pl.ds(m * rows + at, ROWS), g * LANES : (g + 1) * LANES] = total.reshape(
                         ROWS, LANES
                     ).astype(jnp.bfloat16)
@@ -83,8 +85,8 @@
     lax.fori_loop(0, table.shape[0] // COLS, cols, 0)
 
 
-def hole_kernel(modes, nval, ncond, x_ref, c_ref, z_ref, out_ref, table):
-    build_table(x_ref, c_ref, table, modes, nval, ncond, False)
+def hole_kernel(modes, nval, ncond, lower, y_ref, d_ref, z_ref, out_ref, table):
+    build_table(None, None, y_ref, d_ref, table, modes, nval, ncond, lower)
 
     def write(at, got):
         out_ref[:, pl.ds(at, COLS)] = got
@@ -92,7 +94,9 @@
     contract(z_ref, table, write)
 
 
-def elec_kernel(modes, nval, ncond, f_ref, inc_ref, perm_ref, c_ref, z_ref, hole_ref, out_ref, x_ref, table):
+def elec_kernel(
+    modes, nval, ncond, lower, inc_ref, perm_ref, c_ref, y_ref, d_ref, z_ref, hole_ref, out_ref, x_ref, table
+):
     nrow = inc_ref.shape[0]
     wide = inc_ref.shape[2] // nval
     width = perm_ref.shape[1]
@@ -105,11 +109,10 @@
                 preferred_element_type=jnp.float32,
             )
         x_ref[:, v * width : (v + 1) * width] = got.astype(jnp.bfloat16)
-    build_table(x_ref, c_ref, table, modes, nval, ncond, True)
-    factor = f_ref[0]
+    build_table(x_ref, c_ref, y_ref, d_ref, table, modes, nval, ncond, lower)
 
     def write(at, got):
-        out_ref[:, pl.ds(at, COLS)] = (got - hole_ref[:, pl.ds(at, COLS)]) * factor
+        out_ref[:, pl.ds(at, COLS)] = got - hole_ref[:, pl.ds(at, COLS)]
 
     contract(z_ref, table, write)
 
@@ -187,25 +190,18 @@
     whole = jnp.pad(whole.reshape(nrow, kept, depth), ((0, 0), (0, kept_pad - kept), (0, 0)))
     whole = whole.reshape(nrow * kept_pad, depth)
 
-    tops = jnp.stack([jnp.max(jnp.abs(a)).astype(jnp.float32) for a in (coef_zero, coef_shift, coupling)])
-    tops = lax.pmax(tops, ("krow", "exc", "band"))
-    bound = tops[0] * tops[1] * tops[2] * (2.0 * ncond * depth * nrow)
-    factor = 32768.0 / jnp.maximum(bound, 1e-30)
-
     couple = lax.dynamic_slice_in_dim(coupling, half * groups, groups, axis=1).astype(jnp.float32)
     couple = couple.reshape(2, groups, modes * ncond * ncond, 1, kdev)
     couple = jnp.broadcast_to(couple, couple.shape[:3] + (8, kdev))
 
     macs = rows * modes * depth * 4 + whole.shape[0] * cols * depth
     cost = pl.CostEstimate(flops=8 * macs, bytes_accessed=8 * 2**20, transcendentals=0)
-    smem = pl.BlockSpec(memory_space=pltpu.SMEM)
-    vmem = pl.BlockSpec(memory_space=pltpu.VMEM)
     partial_shape = jax.ShapeDtypeStruct((nrow * kept_pad, cols), jnp.float32)
     table = pltpu.VMEM((cols, depth), jnp.bfloat16)
     params = pltpu.CompilerParams(vmem_limit_bytes=LIMIT)
     holes = [
         pl.pallas_call(
-            functools.partial(hole_kernel, modes, nval, ncond),
+            functools.partial(hole_kernel, modes, nval, ncond, lower),
             out_shape=partial_shape,
             scratch_shapes=[table],
             compiler_params=params,
@@ -218,15 +214,13 @@
     pieces = []
     for g in range(groups):
         partial = pl.pallas_call(
-            functools.partial(elec_kernel, modes, nval, ncond),
+            functools.partial(elec_kernel, modes, nval, ncond, lower),
             out_shape=partial_shape,
-            in_specs=[smem] + [vmem] * 5,
-            out_specs=vmem,
             scratch_shapes=[pltpu.VMEM((rows, depth), jnp.bfloat16), table],
             compiler_params=params,
             cost_estimate=cost,
             name="elec",
-        )(factor.reshape(1), incoming[g], perm[g], couple[0, g], whole, holes[g])
+        )(incoming[g], perm[g], couple[0, g], full[g], couple[1, g], whole, holes[g])
         blocks = partial.reshape(nrow, kept_pad, cols)
 
         def block(d):
@@ -238,15 +232,15 @@
             if up is not None:
                 send_up = send_up + up.astype(jnp.float32)
                 send_down = send_down + down.astype(jnp.float32)
-            up = lax.ppermute(send_up.astype(jnp.float16), "krow", [(z, z + 1) for z in range(t)])
+            up = lax.ppermute(send_up.astype(jnp.bfloat16), "krow", [(z, z + 1) for z in range(t)])
             down = lax.ppermute(
-                send_down.astype(jnp.float16), "krow", [(z, z - 1) for z in range(nrow - t, nrow)]
+                send_down.astype(jnp.bfloat16), "krow", [(z, z - 1) for z in range(nrow - t, nrow)]
             )
         total = block(me)
         if up is not None:
             total = total + up.astype(jnp.float32) + down.astype(jnp.float32)
         total = total[:kept, : modes * rows].reshape(kept, modes, rows)[:, :, :share]
-        pieces.append(total * (scale / factor))
+        pieces.append(total * scale)
     return jnp.stack(pieces, axis=1)
 
 

time: 233 us -> 201 us (0.86)
  blocking collectives: 33.2 us -> 0 us
  other arithmetic: 25.6 us -> 14 us
  local copies, waits for them, and re-layouts: 58.4 us -> 64.5 us
  waiting for transfers between devices: 24.7 us -> 29.7 us
  Pallas kernels: 44.9 us -> 48.6 us
    pmax x1 -> x0, blocking collectives: 33.2 us -> none  [local(): tops = lax.pmax(tops, ('krow', 'exc', 'band'))]
    ppermute x1, waiting for transfers between devices: 0.01 us -> 6.88 us  [local(): other = lax.ppermute(zero, 'exc', [(0, 1), (1, 0)])]
    reduce_max x3 -> x0, other arithmetic: 5.71 us -> none  [local(): jnp.max(jnp.abs(a)).astype(jnp.float32)]
    unnamed x62 -> x80, local copies, waits for them, and re-layouts: 18.7 us -> 22.5 us
    pallas_call x4, Pallas kernels: 41 us -> 44.7 us  [the longest x2 28.5 us: local(): pl.pallas_call(functools.partial(elec_kernel, modes, nval, ncond, lower),...]
    ppermute x12, waiting for transfers between devices: 24.7 us -> 21.4 us  [the longest x6 21.4 us: local(): lax.ppermute(send_up.astype(jnp.bfloat16), 'krow', [(z, z + 1) for z in r...]
    convert_element_type x12 -> x8, other arithmetic: 8.54 us -> 5.35 us  [the longest x4 2.89 us: local(): send_up.astype(jnp.bfloat16)]
    dynamic_slice x11 -> x12, local copies, waits for them, and re-layouts: 21.2 us -> 23.7 us  [block(): lax.dynamic_index_in_dim(blocks, jnp.clip(d, 0, nrow - 1), axis=0, keepdi...]
  transfers between devices with their start and end apart: 16 -> 16, of which waited for: 5 -> 6; matrix products, arithmetic and copies ran while one was open for 27% -> 28% of each run, Pallas kernels for 14% -> 16%
where the time goes in v2:
time: 201 us; the launch traced here: 197 us
  local copies, waits for them, and re-layouts  64.5 us (32%)
  Pallas kernels  48.6 us (24%)
  starting transfers between devices  39.2 us (20%)
  waiting for transfers between devices  29.7 us (15%)
  other arithmetic  14 us (7%)
    pallas_call x2, Pallas kernels, local(): pl.pallas_call(functools.partial(elec_kernel, modes, nval, ncond, lower),...  28.5 us
    dynamic_slice x12, local copies, waits for them, and re-layouts, block(): lax.dynamic_index_in_dim(blocks, jnp.clip(d, 0, nrow - 1), axis=0, keepdi...  23.7 us
    unnamed x80, local copies, waits for them, and re-layouts  22.5 us
    ppermute x6, waiting for transfers between devices, local(): lax.ppermute(send_up.astype(jnp.bfloat16), 'krow', [(z, z + 1) for z in r...  21.4 us
    ppermute x6, starting transfers between devices, local(): lax.ppermute(send_up.astype(jnp.bfloat16), 'krow', [(z, z + 1) for z in r...  19.3 us
    pallas_call x2, Pallas kernels, local(): pl.pallas_call(functools.partial(hole_kernel, modes, nval, ncond, lower),...  16.2 us
    all_to_all x2, starting transfers between devices, local(): lax.all_to_all(outgoing, 'krow', split_axis=0, concat_axis=0, tiled=True)  9.51 us
    ppermute x6, starting transfers between devices, local(): lax.ppermute(send_down.astype(jnp.bfloat16), 'krow', [(z, z - 1) for z in...  6.99 us
  transfers between devices with their start and end apart: 16, of which 6 were waited for; matrix products, arithmetic and copies ran while one was open for 28% of the time, Pallas kernels for 16%

profile of v2, /device:TPU:0, one launch (start us, length us, event | category | flops | bytes accessed | tf_op | source)
XLA Modules:
  0.0 197.4 jit_solution(14465343429397285714)
XLA Ops:
  0.0 3.0 %reshape.74 = bf16[4,200,1024]{2,1,0:T(8,128)(2,1)S(1)} reshape(bf16[4,200,2,4,128]{4,3,2,1,0:T(4,128)(2,1)} %param.5) | data formatting | bytes 3276800 | tf_op jit(solution)/shard_map/reshape | solution.py:141
  6.0 2.9 %collective-permute-start.1 = (bf16[200,2048]{1,0:T(8,128)(2,1)}, bf16[200,2048]{1,0:T(8,128)(2,1)}, u32[]{:S(2)}, u32[]{:S(2)}) collective-permute-start(bf16[200,2048]{1,0:T(8,128)(2,1)} %reshape.76), channel_id=1, source_target_pairs={{0,2},{2,0},{1,3},{3,1},{4,6},{6,4},{5,7},{7,5},{8,10},{10,8},{9,1... | collective-permute-start | bytes 2457608 | tf_op jit(solution)/shard_map/ppermute | solution.py:185
  18.2 2.0 copy.33
  20.8 6.9 %collective-permute-done.1 = bf16[200,2048]{1,0:T(8,128)(2,1)} collective-permute-done((bf16[200,2048]{1,0:T(8,128)(2,1)}, bf16[200,2048]{1,0:T(8,128)(2,1)}, u32[]{:S(2)}, u32[]{:S(2)}) %collective-permute-start.1) | collective-permute-done | bytes 819232 | tf_op jit(solution)/shard_map/ppermute | solution.py:185
  27.7 2.7 %broadcast_select_fusion.3 = (bf16[200,2048]{1,0:T(8,128)(2,1)}, bf16[200,2048]{1,0:T(8,128)(2,1)}) fusion(bf16[200,2048]{1,0:T(8,128)(2,1)} %reshape.76, bf16[200,2048]{1,0:T(8,128)(2,1)} %collective-permute-done.1, pred[]{:T(512)S(6)} %eq.110), kind=kLoop, calls=%fused_computation.42 | loop fusion | flops 819200 | bytes 3276801 | tf_op jit(solution)/shard_map/jit(_where)/select_n | solution.py:187
  32.1 2.0 pick.2
  34.0 5.1 %all-to-all-start = ((bf16[4,208,512]{2,1,0:T(8,128)(2,1)}), bf16[4,208,512]{2,1,0:T(8,128)(2,1)}, u32[]{:S(2)}, u32[]{:S(2)}) async-start(bf16[4,208,512]{2,1,0:T(8,128)(2,1)} %pick.2), calls=%async_computation | async-start | bytes 1703936 | tf_op jit(solution)/shard_map/all_to_all | solution.py:181
  39.2 2.8 %pad_maximum_fusion.1 = bf16[400,2048]{1,0:T(8,128)(2,1)} fusion(bf16[200,2048]{1,0:T(8,128)(2,1)} %get-tuple-element.24, bf16[200,2048]{1,0:T(8,128)(2,1)} %get-tuple-element.23), kind=kLoop, calls=%fused_computation.3 | loop fusion | flops 3276800 | bytes 3276800 | tf_op jit(solution)/shard_map/concatenate | solution.py:187
  42.0 2.5 %reshape.77 = bf16[4,100,2048]{2,1,0:T(8,128)(2,1)} reshape(bf16[400,2048]{1,0:T(8,128)(2,1)} %pad_maximum_fusion.1) | data formatting | bytes 3276800 | tf_op jit(solution)/shard_map/reshape | solution.py:190
  48.1 8.1 %hole.2.hole_ref = f32[416,1920]{1,0:T(8,128)S(1)} custom-call(bf16[208,2048]{1,0:T(8,128)(2,1)S(1)} %get-tuple-element.21.x_ref.y_ref, f32[144,8,128]{2,1,0:T(8,128)S(1)} %broadcast_in_dim.42.d_ref, bf16[416,2048]{1,0:T(8,128)(2,1)S(1)} %bitcast.95), custom_call_target="tpu_custom_call" | custom-call | flops 13208911872 | bytes 8388608 | tf_op jit(solution)/shard_map/hole/pallas_call | solution.py:203
  60.2 4.4 %all-to-all-start.1 = ((bf16[4,208,512]{2,1,0:T(8,128)(2,1)}), bf16[4,208,512]{2,1,0:T(8,128)(2,1)}, u32[]{:S(2)}, u32[]{:S(2)}) async-start(bf16[4,208,512]{2,1,0:T(8,128)(2,1)} %pick.3), calls=%async_computation.1 | async-start | bytes 1703936 | tf_op jit(solution)/shard_map/all_to_all | solution.py:181
  64.7 8.1 %hole.3.hole_ref = f32[416,1920]{1,0:T(8,128)S(1)} custom-call(bf16[208,2048]{1,0:T(8,128)(2,1)S(1)} %get-tuple-element.22.x_ref.y_ref, f32[144,8,128]{2,1,0:T(8,128)S(1)} %broadcast_in_dim.46.d_ref, bf16[416,2048]{1,0:T(8,128)(2,1)S(1)} %bitcast.96), custom_call_target="tpu_custom_call" | custom-call | flops 13208911872 | bytes 8388608 | tf_op jit(solution)/shard_map/hole/pallas_call | solution.py:203
  74.5 14.2 %elec.2 = f32[416,1920]{1,0:T(8,128)S(1)} custom-call(bf16[4,208,512]{2,1,0:T(8,128)(2,1)} %all-to-all-done.inc_ref, bf16[512,512]{1,0:T(8,128)(2,1)S(1)} %bitcast.100, f32[144,8,128]{2,1,0:T(8,128)S(1)} %broadcast_in_dim.40.c_ref, bf16[208,2048]{1,0:T(8,128)(2,1)S(1)} %copy-done.6, f32[144,8,128]{2,1,0:T(8,128)S(1)} %copy-done.14, ...), custom_call_target="tpu_custom_call" | custom-call | flops 13208911872 | bytes 8388608 | tf_op jit(solution)/shard_map/elec/pallas_call | solution.py:216
  95.5 14.2 %elec.3 = f32[416,1920]{1,0:T(8,128)S(1)} custom-call(bf16[4,208,512]{2,1,0:T(8,128)(2,1)} %all-to-all-done.1.inc_ref, bf16[512,512]{1,0:T(8,128)(2,1)S(1)} %bitcast.99, f32[144,8,128]{2,1,0:T(8,128)S(1)} %broadcast_in_dim.44.c_ref, bf16[208,2048]{1,0:T(8,128)(2,1)S(1)} %copy-done.4, f32[144,8,128]{2,1,0:T(8,128)S(1)} %copy-done.12, ...), custom_call_target="tpu_custom_call" | custom-call | flops 13208911872 | bytes 8388608 | tf_op jit(solution)/shard_map/elec/pallas_call | solution.py:216
  112.6 2.0 %copy.25 = bf16[1,104,1920]{1,2,0:T(8,128)(2,1)} copy(bf16[1,104,1920]{2,1,0:T(8,128)(2,1)} %get-tuple-element.41) | data formatting | bytes 798720
  114.6 4.5 %collective-permute-start.2 = (bf16[104,1920]{0,1:T(8,128)(2,1)}, bf16[104,1920]{0,1:T(8,128)(2,1)}, u32[]{:S(2)}, u32[]{:S(2)}) collective-permute-start(bf16[104,1920]{0,1:T(8,128)(2,1)} %bitcast.108), channel_id=1, source_target_pairs={{0,4},{1,5},{2,6},{3,7},{16,20},{17,21},{18,22},{19,23}} | collective-permute-start | bytes 1198088 | tf_op jit(solution)/shard_map/ppermute | solution.py:235
  119.1 5.4 %constant_dynamic-slice_fusion.4 = (f32[1,104,1920]{2,1,0:T(8,128)}, f32[1,104,1920]{2,1,0:T(8,128)}, f32[1,104,1920]{2,1,0:T(8,128)}, f32[1,104,1920]{2,1,0:T(8...) fusion(f32[4,104,1920]{2,1,0:T(8,128)} %bitcast.94, ...), kind=kLoop, calls=%fused_computation.75 | loop fusion | bytes 15974420 | tf_op jit(solution)/shard_map/jit(dynamic_index_in_dim)/dynamic_slice | solution.py:227
  124.5 2.5 %copy.11 = f32[1,104,1920]{1,2,0:T(8,128)} copy(f32[1,104,1920]{2,1,0:T(8,128)} %get-tuple-element.39) | data formatting | bytes 1597440 | tf_op jit(solution)/shard_map/jit(dynamic_index_in_dim)/dynamic_slice | solution.py:227
  131.5 2.5 %copy.9 = f32[1,104,1920]{1,2,0:T(8,128)} copy(f32[1,104,1920]{2,1,0:T(8,128)} %get-tuple-element.35) | data formatting | bytes 1597440 | tf_op jit(solution)/shard_map/jit(dynamic_index_in_dim)/dynamic_slice | solution.py:227
  135.1 2.1 %collective-permute-start.8 = (bf16[104,1920]{0,1:T(8,128)(2,1)}, bf16[104,1920]{0,1:T(8,128)(2,1)}, u32[]{:S(2)}, u32[]{:S(2)}) collective-permute-start(bf16[104,1920]{0,1:T(8,128)(2,1)} %bitcast.110), channel_id=1, source_target_pairs={{0,4},{1,5},{2,6},{3,7},{16,20},{17,21},{18,22},{19,23}} | collective-permute-start | bytes 1198088 | tf_op jit(solution)/shard_map/ppermute | solution.py:235
  139.9 2.0 %copy.28 = bf16[1,104,1920]{1,2,0:T(8,128)(2,1)} copy(bf16[1,104,1920]{2,1,0:T(8,128)(2,1)} %get-tuple-element.13) | data formatting | bytes 798720
  143.4 2.5 %copy.22 = f32[1,104,1920]{1,2,0:T(8,128)} copy(f32[1,104,1920]{2,1,0:T(8,128)} %get-tuple-element.15) | data formatting | bytes 1597440 | tf_op jit(solution)/shard_map/jit(dynamic_index_in_dim)/dynamic_slice | solution.py:227
  145.9 2.4 %copy.21 = f32[1,104,1920]{1,2,0:T(8,128)} copy(f32[1,104,1920]{2,1,0:T(8,128)} %get-tuple-element.16) | data formatting | bytes 1597440 | tf_op jit(solution)/shard_map/jit(dynamic_index_in_dim)/dynamic_slice | solution.py:227
  148.3 2.4 %copy.17 = f32[1,104,1920]{1,2,0:T(8,128)} copy(f32[1,104,1920]{2,1,0:T(8,128)} %get-tuple-element.18) | data formatting | bytes 1597440 | tf_op jit(solution)/shard_map/jit(dynamic_index_in_dim)/dynamic_slice | solution.py:227
  156.8 2.3 %collective-permute-start.9 = (bf16[104,1920]{0,1:T(8,128)(2,1)S(1)}, bf16[104,1920]{0,1:T(8,128)(2,1)S(1)}, u32[]{:S(2)}, u32[]{:S(2)}) collective-permute-start(bf16[104,1920]{0,1:T(8,128)(2,1)S(1)} %fusion.4), channel_id=1, source_target_pairs={{0,4},{4,8},{1,5},{5,9},{2,6},{6,10},{3,7},{7,11},{16,20},{20,24},... | collective-permute-start | bytes 1198088 | tf_op jit(solution)/shard_map/ppermute | solution.py:235
  161.0 4.4 %collective-permute-done.3 = bf16[104,1920]{0,1:T(8,128)(2,1)S(1)} collective-permute-done((bf16[104,1920]{0,1:T(8,128)(2,1)S(1)}, bf16[104,1920]{0,1:T(8,128)(2,1)S(1)}, u32[]{:S(2)}, u32[]{:S(2)}) %collective-permute-start.3) | collective-permute-done | bytes 399392 | tf_op jit(solution)/shard_map/ppermute | solution.py:235
  165.5 4.5 %collective-permute-start.4 = (bf16[104,1920]{0,1:T(8,128)(2,1)S(1)}, bf16[104,1920]{0,1:T(8,128)(2,1)S(1)}, u32[]{:S(2)}, u32[]{:S(2)}) collective-permute-start(bf16[104,1920]{0,1:T(8,128)(2,1)S(1)} %fusion.9), channel_id=1, source_target_pairs={{0,4},{4,8},{8,12},{1,5},{5,9},{9,13},{2,6},{6,10},{10,14},{3,7},{... | collective-permute-start | bytes 1198088 | tf_op jit(solution)/shard_map/ppermute | solution.py:235
  171.6 4.3 %collective-permute-done.9 = bf16[104,1920]{0,1:T(8,128)(2,1)S(1)} collective-permute-done((bf16[104,1920]{0,1:T(8,128)(2,1)S(1)}, bf16[104,1920]{0,1:T(8,128)(2,1)S(1)}, u32[]{:S(2)}, u32[]{:S(2)}) %collective-permute-start.9) | collective-permute-done | bytes 399392 | tf_op jit(solution)/shard_map/ppermute | solution.py:235
  176.0 4.4 %collective-permute-start.10 = (bf16[104,1920]{0,1:T(8,128)(2,1)S(1)}, bf16[104,1920]{0,1:T(8,128)(2,1)S(1)}, u32[]{:S(2)}, u32[]{:S(2)}) collective-permute-start(bf16[104,1920]{0,1:T(8,128)(2,1)S(1)} %fusion.5), channel_id=1, source_target_pairs={{0,4},{4,8},{8,12},{1,5},{5,9},{9,13},{2,6},{6,10},{10,14},{3,7},{... | collective-permute-start | bytes 1198088 | tf_op jit(solution)/shard_map/ppermute | solution.py:235
  181.9 4.6 %collective-permute-done.4 = bf16[104,1920]{0,1:T(8,128)(2,1)S(1)} collective-permute-done((bf16[104,1920]{0,1:T(8,128)(2,1)S(1)}, bf16[104,1920]{0,1:T(8,128)(2,1)S(1)}, u32[]{:S(2)}, u32[]{:S(2)}) %collective-permute-start.4) | collective-permute-done | bytes 399392 | tf_op jit(solution)/shard_map/ppermute | solution.py:235
  186.7 8.0 %collective-permute-done.10 = bf16[104,1920]{0,1:T(8,128)(2,1)S(1)} collective-permute-done((bf16[104,1920]{0,1:T(8,128)(2,1)S(1)}, bf16[104,1920]{0,1:T(8,128)(2,1)S(1)}, u32[]{:S(2)}, u32[]{:S(2)}) %collective-permute-start.10) | collective-permute-done | bytes 399392 | tf_op jit(solution)/shard_map/ppermute | solution.py:235
  195.1 2.3 %copy.24 = f32[100,2,9,200]{3,1,2,0:T(2,128)} copy(f32[100,2,9,200]{0,3,2,1:T(8,128)S(1)} %pad_maximum_fusion) | data formatting | bytes 2880000 | tf_op jit(solution)/shard_map/stack | solution.py:244
  (148 shorter events, 54.5 us)
Async XLA Ops:
  0.0 13.9 %copy-start = (bf16[2,4,9,4,4,128]{5,4,3,2,1,0:T(4,128)(2,1)S(1)}, bf16[2,4,9,4,4,128]{5,4,3,2,1,0:T(4,128)(2,1)}, u32[]{:S(2)}) copy-start(bf16[2,4,9,4,4,128]{5,4,3,2,1,0:T(4,128)(2,1)} %param.6) | copy-start | bytes 884740
  3.0 5.9 %copy-start.36 = (s32[4,512]{1,0:T(4,128)S(1)}, s32[4,512]{1,0:T(4,128)}, u32[]{:S(2)}) copy-start(s32[4,512]{1,0:T(4,128)} %param.7) | copy-start | bytes 24580
  4.0 26.4 %collective-permute-start = (bf16[2,208,1024]{2,1,0:T(8,128)(2,1)}, bf16[2,208,1024]{2,1,0:T(8,128)(2,1)}, u32[]{:S(2)}, u32[]{:S(2)}) collective-permute-start(bf16[2,208,1024]{2,1,0:T(8,128)(2,1)} %pad_dynamic-slice_fusion), channel_id=1, source_target_pairs={{0,1},{1,0},{2,3},{3,2},{4,5},{5,4},{6,7},{7,6},{8,9},{9,8},{10,11... | collective-permute-start | bytes 2555912 | tf_op jit(solution)/shard_map/ppermute | solution.py:144
  6.0 21.7 %collective-permute-start.1 = (bf16[200,2048]{1,0:T(8,128)(2,1)}, bf16[200,2048]{1,0:T(8,128)(2,1)}, u32[]{:S(2)}, u32[]{:S(2)}) collective-permute-start(bf16[200,2048]{1,0:T(8,128)(2,1)} %reshape.76), channel_id=1, source_target_pairs={{0,2},{2,0},{1,3},{3,1},{4,6},{6,4},{5,7},{7,5},{8,10},{10,8},{9,1... | collective-permute-start | bytes 2457608 | tf_op jit(solution)/shard_map/ppermute | solution.py:185
  32.1 16.0 %copy-start.5 = (bf16[208,2048]{1,0:T(8,128)(2,1)}, bf16[208,2048]{1,0:T(8,128)(2,1)S(1)}, u32[]{:S(2)}) copy-start(bf16[208,2048]{1,0:T(8,128)(2,1)S(1)} %get-tuple-element.21.x_ref.y_ref) | copy-start | bytes 2555908
  32.1 32.5 %copy-start.3 = (bf16[208,2048]{1,0:T(8,128)(2,1)}, bf16[208,2048]{1,0:T(8,128)(2,1)S(1)}, u32[]{:S(2)}) copy-start(bf16[208,2048]{1,0:T(8,128)(2,1)S(1)} %get-tuple-element.22.x_ref.y_ref) | copy-start | bytes 2555908
  34.0 26.1 %all-to-all-start = ((bf16[4,208,512]{2,1,0:T(8,128)(2,1)}), bf16[4,208,512]{2,1,0:T(8,128)(2,1)}, u32[]{:S(2)}, u32[]{:S(2)}) async-start(bf16[4,208,512]{2,1,0:T(8,128)(2,1)} %pick.2), calls=%async_computation | async-start | bytes 1703936 | tf_op jit(solution)/shard_map/all_to_all | solution.py:181
  58.7 5.9 %copy-start.8 = (bf16[4,104,2048]{2,1,0:T(8,128)(2,1)S(1)}, bf16[4,104,2048]{2,1,0:T(8,128)(2,1)}, u32[]{:S(2)}) copy-start(bf16[4,104,2048]{2,1,0:T(8,128)(2,1)} %copy-done.7) | copy-start | bytes 5111812
  60.2 28.6 %all-to-all-start.1 = ((bf16[4,208,512]{2,1,0:T(8,128)(2,1)}), bf16[4,208,512]{2,1,0:T(8,128)(2,1)}, u32[]{:S(2)}, u32[]{:S(2)}) async-start(bf16[4,208,512]{2,1,0:T(8,128)(2,1)} %pick.3), calls=%async_computation.1 | async-start | bytes 1703936 | tf_op jit(solution)/shard_map/all_to_all | solution.py:181
  64.6 8.2 %copy-start.11 = (f32[144,8,128]{2,1,0:T(8,128)}, f32[144,8,128]{2,1,0:T(8,128)S(1)}, u32[]{:S(2)}) copy-start(f32[144,8,128]{2,1,0:T(8,128)S(1)} %broadcast_in_dim.46.d_ref) | copy-start | bytes 1769476
  64.6 9.9 %copy-start.6 = (bf16[208,2048]{1,0:T(8,128)(2,1)S(1)}, bf16[208,2048]{1,0:T(8,128)(2,1)}, u32[]{:S(2)}) copy-start(bf16[208,2048]{1,0:T(8,128)(2,1)} %copy-done.5) | copy-start | bytes 2555908
  64.6 9.9 %copy-start.9 = (bf16[4,104,2048]{2,1,0:T(8,128)(2,1)S(1)}, bf16[4,104,2048]{2,1,0:T(8,128)(2,1)}, u32[]{:S(2)}) copy-start(bf16[4,104,2048]{2,1,0:T(8,128)(2,1)} %copy-done.7) | copy-start | bytes 5111812
  64.7 9.9 %copy-start.14 = (f32[144,8,128]{2,1,0:T(8,128)S(1)}, f32[144,8,128]{2,1,0:T(8,128)}, u32[]{:S(2)}) copy-start(f32[144,8,128]{2,1,0:T(8,128)} %copy-done.13) | copy-start | bytes 1769476
  64.7 9.9 %copy-start.16 = (bf16[64,8,4,128]{3,1,2,0:T(8,128)(2,1)S(1)}, bf16[64,8,4,128]{3,1,2,0:T(8,128)(2,1)}, u32[]{:S(2)}) copy-start(bf16[64,8,4,128]{3,1,2,0:T(8,128)(2,1)} %copy.34) | copy-start | bytes 1572868
  64.7 9.9 %copy-start.20 = (f32[416,1920]{1,0:T(8,128)S(1)}, f32[416,1920]{1,0:T(8,128)}, u32[]{:S(2)}) copy-start(f32[416,1920]{1,0:T(8,128)} %copy-done.19) | copy-start | bytes 9584644
  74.5 14.3 %copy-start.35 = (f32[144,128]{1,0:T(8,128)S(1)}, f32[144,128]{1,0:T(8,128)}, u32[]{:S(2)}) copy-start(f32[144,128]{1,0:T(8,128)} %get-tuple-element.31) | copy-start | bytes 221188
  114.6 36.2 %collective-permute-start.2 = (bf16[104,1920]{0,1:T(8,128)(2,1)}, bf16[104,1920]{0,1:T(8,128)(2,1)}, u32[]{:S(2)}, u32[]{:S(2)}) collective-permute-start(bf16[104,1920]{0,1:T(8,128)(2,1)} %bitcast.108), channel_id=1, source_target_pairs={{0,4},{1,5},{2,6},{3,7},{16,20},{17,21},{18,22},{19,23}} | collective-permute-start | bytes 1198088 | tf_op jit(solution)/shard_map/ppermute | solution.py:235
  128.4 25.4 %collective-permute-start.5 = (bf16[104,1920]{0,1:T(8,128)(2,1)}, bf16[104,1920]{0,1:T(8,128)(2,1)}, u32[]{:S(2)}, u32[]{:S(2)}) collective-permute-start(bf16[104,1920]{0,1:T(8,128)(2,1)} %bitcast.109), channel_id=1, source_target_pairs={{12,8},{13,9},{14,10},{15,11},{28,24},{29,25},{30,26},{31,27}} | collective-permute-start | bytes 1198088 | tf_op jit(solution)/shard_map/ppermute | solution.py:236
  135.1 20.5 %collective-permute-start.8 = (bf16[104,1920]{0,1:T(8,128)(2,1)}, bf16[104,1920]{0,1:T(8,128)(2,1)}, u32[]{:S(2)}, u32[]{:S(2)}) collective-permute-start(bf16[104,1920]{0,1:T(8,128)(2,1)} %bitcast.110), channel_id=1, source_target_pairs={{0,4},{1,5},{2,6},{3,7},{16,20},{17,21},{18,22},{19,23}} | collective-permute-start | bytes 1198088 | tf_op jit(solution)/shard_map/ppermute | solution.py:235
  142.0 17.2 %collective-permute-start.11 = (bf16[104,1920]{0,1:T(8,128)(2,1)}, bf16[104,1920]{0,1:T(8,128)(2,1)}, u32[]{:S(2)}, u32[]{:S(2)}) collective-permute-start(bf16[104,1920]{0,1:T(8,128)(2,1)} %bitcast.111), channel_id=1, source_target_pairs={{12,8},{13,9},{14,10},{15,11},{28,24},{29,25},{30,26},{31,27}} | collective-permute-start | bytes 1198088 | tf_op jit(solution)/shard_map/ppermute | solution.py:236
  152.3 6.8 %copy-start.24 = (f32[1,104,1920]{1,2,0:T(8,128)S(1)}, f32[1,104,1920]{1,2,0:T(8,128)}, u32[]{:S(2)}) copy-start(f32[1,104,1920]{1,2,0:T(8,128)} %copy.22) | copy-start | bytes 2396164
  152.3 13.1 %collective-permute-start.3 = (bf16[104,1920]{0,1:T(8,128)(2,1)S(1)}, bf16[104,1920]{0,1:T(8,128)(2,1)S(1)}, u32[]{:S(2)}, u32[]{:S(2)}) collective-permute-start(bf16[104,1920]{0,1:T(8,128)(2,1)S(1)} %fusion.8), channel_id=1, source_target_pairs={{0,4},{4,8},{1,5},{5,9},{2,6},{6,10},{3,7},{7,11},{16,20},{20,24},... | collective-permute-start | bytes 1198088 | tf_op jit(solution)/shard_map/ppermute | solution.py:235
  154.9 15.1 %collective-permute-start.6 = (bf16[104,1920]{0,1:T(8,128)(2,1)S(1)}, bf16[104,1920]{0,1:T(8,128)(2,1)S(1)}, u32[]{:S(2)}, u32[]{:S(2)}) collective-permute-start(bf16[104,1920]{0,1:T(8,128)(2,1)S(1)} %fusion.6), channel_id=1, source_target_pairs={{8,4},{12,8},{9,5},{13,9},{10,6},{14,10},{11,7},{15,11},{24,20},{2... | collective-permute-start | bytes 1198088 | tf_op jit(solution)/shard_map/ppermute | solution.py:236
  156.8 19.2 %collective-permute-start.9 = (bf16[104,1920]{0,1:T(8,128)(2,1)S(1)}, bf16[104,1920]{0,1:T(8,128)(2,1)S(1)}, u32[]{:S(2)}, u32[]{:S(2)}) collective-permute-start(bf16[104,1920]{0,1:T(8,128)(2,1)S(1)} %fusion.4), channel_id=1, source_target_pairs={{0,4},{4,8},{1,5},{5,9},{2,6},{6,10},{3,7},{7,11},{16,20},{20,24},... | collective-permute-start | bytes 1198088 | tf_op jit(solution)/shard_map/ppermute | solution.py:235
  160.3 20.2 %collective-permute-start.12 = (bf16[104,1920]{0,1:T(8,128)(2,1)S(1)}, bf16[104,1920]{0,1:T(8,128)(2,1)S(1)}, u32[]{:S(2)}, u32[]{:S(2)}) collective-permute-start(bf16[104,1920]{0,1:T(8,128)(2,1)S(1)} %fusion.2), channel_id=1, source_target_pairs={{8,4},{12,8},{9,5},{13,9},{10,6},{14,10},{11,7},{15,11},{24,20},{2... | collective-permute-start | bytes 1198088 | tf_op jit(solution)/shard_map/ppermute | solution.py:236
  165.5 15.0 %copy-start.21 = (f32[1,104,1920]{1,2,0:T(8,128)S(1)}, f32[1,104,1920]{1,2,0:T(8,128)}, u32[]{:S(2)}) copy-start(f32[1,104,1920]{1,2,0:T(8,128)} %copy.21) | copy-start | bytes 2396164
  165.5 21.0 %collective-permute-start.4 = (bf16[104,1920]{0,1:T(8,128)(2,1)S(1)}, bf16[104,1920]{0,1:T(8,128)(2,1)S(1)}, u32[]{:S(2)}, u32[]{:S(2)}) collective-permute-start(bf16[104,1920]{0,1:T(8,128)(2,1)S(1)} %fusion.9), channel_id=1, source_target_pairs={{0,4},{4,8},{8,12},{1,5},{5,9},{9,13},{2,6},{6,10},{10,14},{3,7},{... | collective-permute-start | bytes 1198088 | tf_op jit(solution)/shard_map/ppermute | solution.py:235
  170.2 16.3 %copy-start.25 = (f32[1,104,1920]{1,2,0:T(8,128)S(1)}, f32[1,104,1920]{1,2,0:T(8,128)}, u32[]{:S(2)}) copy-start(f32[1,104,1920]{1,2,0:T(8,128)} %copy.9) | copy-start | bytes 2396164
  170.2 16.3 %collective-permute-start.7 = (bf16[104,1920]{0,1:T(8,128)(2,1)S(1)}, bf16[104,1920]{0,1:T(8,128)(2,1)S(1)}, u32[]{:S(2)}, u32[]{:S(2)}) collective-permute-start(bf16[104,1920]{0,1:T(8,128)(2,1)S(1)} %fusion.7), channel_id=1, source_target_pairs={{4,0},{8,4},{12,8},{5,1},{9,5},{13,9},{6,2},{10,6},{14,10},{7,3},{... | collective-permute-start | bytes 1198088 | tf_op jit(solution)/shard_map/ppermute | solution.py:236
  176.0 18.7 %collective-permute-start.10 = (bf16[104,1920]{0,1:T(8,128)(2,1)S(1)}, bf16[104,1920]{0,1:T(8,128)(2,1)S(1)}, u32[]{:S(2)}, u32[]{:S(2)}) collective-permute-start(bf16[104,1920]{0,1:T(8,128)(2,1)S(1)} %fusion.5), channel_id=1, source_target_pairs={{0,4},{4,8},{8,12},{1,5},{5,9},{9,13},{2,6},{6,10},{10,14},{3,7},{... | collective-permute-start | bytes 1198088 | tf_op jit(solution)/shard_map/ppermute | solution.py:235
  180.6 14.1 %collective-permute-start.13 = (bf16[104,1920]{0,1:T(8,128)(2,1)S(1)}, bf16[104,1920]{0,1:T(8,128)(2,1)S(1)}, u32[]{:S(2)}, u32[]{:S(2)}) collective-permute-start(bf16[104,1920]{0,1:T(8,128)(2,1)S(1)} %fusion.3), channel_id=1, source_target_pairs={{4,0},{8,4},{12,8},{5,1},{9,5},{13,9},{6,2},{10,6},{14,10},{7,3},{... | collective-permute-start | bytes 1198088 | tf_op jit(solution)/shard_map/ppermute | solution.py:236
  186.5 8.3 %copy-start.26 = (f32[1,104,1920]{1,2,0:T(8,128)S(1)}, f32[1,104,1920]{1,2,0:T(8,128)}, u32[]{:S(2)}) copy-start(f32[1,104,1920]{1,2,0:T(8,128)} %copy.17) | copy-start | bytes 2396164
  (21 other events, 50.4 us)

commit v3 on v2

v3 whole, which is shorter than its diff:
```python
import functools

import jax
import jax.numpy as jnp
from jax import lax
from jax.experimental import pallas as pl
from jax.experimental.pallas import tpu as pltpu
from jax.sharding import PartitionSpec as P

PEERS = 4
ROWS = 16
LANES = 128
COLS = 384
LIMIT = 56 * 2**20
MESH = pl.DeviceIdType.MESH


def round_up(n, unit):
    return (n + unit - 1) // unit * unit


def build_table(x_ref, c_ref, y_ref, d_ref, table, modes, nval, ncond, lower):
    rows = y_ref.shape[1]

    def chunk(r, carry):
        at = pl.multiple_of(r * ROWS, ROWS)

        def slab(ref, g):
            piece = ref[pl.ds(at, ROWS), g * LANES : (g + 1) * LANES]
            return piece.astype(jnp.float32).reshape(ROWS // 8, 8, LANES)

        for v in range(nval):
            own = [w for w in range(nval) if (w // lower == v // lower) == (x_ref is not None)]
            if x_ref is not None:
                shifted = [slab(x_ref, v * ncond + a) for a in range(ncond)]
            for c in range(ncond):
                held = [slab(y_ref.at[w // lower], w % lower * ncond + c) for w in own]
                for m in range(modes):
                    total = None
                    for w, one in zip(own, held):
                        term = one * d_ref[(m * nval + v) * nval + w][None]
                        total = term if total is None else total + term
                    if x_ref is not None:
                        elec = None
                        for a in range(ncond):
                            term = shifted[a] * c_ref[(m * ncond + a) * ncond + c][None]
                            elec = term if elec is None else elec + term
                        total = elec - total
                    g = v * ncond + c
                    table[pl.ds(m * rows + at, ROWS), g * LANES : (g + 1) * LANES] = total.reshape(
                        ROWS, LANES
                    ).astype(jnp.bfloat16)
        return carry

    lax.fori_loop(0, rows // ROWS, chunk, 0)
    used = modes * rows
    if used < table.shape[0]:
        table[used:, :] = jnp.zeros((table.shape[0] - used, table.shape[1]), jnp.bfloat16)


def contract(z_ref, table, write):
    def cols(j, carry):
        at = pl.multiple_of(j * COLS, COLS)
        write(
            at,
            lax.dot_general(
                z_ref[...],
                table[pl.ds(at, COLS), :],
                (((1,), (1,)), ((), ())),
                preferred_element_type=jnp.float32,
            ),
        )
        return carry

    lax.fori_loop(0, table.shape[0] // COLS, cols, 0)


def main_kernel(
    dims, zero_ref, flat_ref, sel_ref, perm_ref, c_ref, d_ref, out_ref,
    zbuf, full, outgo, inc, x_ref, table, part, up_out, up_in, down_out, down_in,
    local_sem, band_sem, exc_send, exc_recv, go_send, go_recv, up_send, up_recv, down_send, down_recv,
):
    modes, nval, ncond, lower, groups, kept_pad, nrow, nexc, scale = dims
    me, exc, half = lax.axis_index("krow"), lax.axis_index("exc"), lax.axis_index("band")
    width, wide = sel_ref.shape[2:]
    zrows = zero_ref.shape[0]
    last = nrow - 1

    barrier = pltpu.get_barrier_semaphore()
    for s in range(1, nrow):
        pl.semaphore_signal(barrier, inc=1, device_id={"krow": lax.rem(me + s, nrow)}, device_id_type=MESH)
    for s in range(1, nexc):
        pl.semaphore_signal(barrier, inc=1, device_id={"exc": lax.rem(exc + s, nexc)}, device_id_type=MESH)
    pl.semaphore_signal(barrier, inc=1, device_id={"band": 1 - half}, device_id_type=MESH)
    pl.semaphore_wait(barrier, nrow - 1 + nexc - 1 + 1)

    own_full = pltpu.make_async_copy(flat_ref.at[pl.ds(half * groups, groups)], full.at[half], local_sem.at[0])
    band_copy = pltpu.make_async_remote_copy(
        src_ref=flat_ref.at[pl.ds((1 - half) * groups, groups)],
        dst_ref=full.at[half],
        send_sem=band_sem.at[0],
        recv_sem=band_sem.at[1],
        device_id={"band": 1 - half},
        device_id_type=MESH,
    )
    band_copy.start()
    own_full.start()
    place = pl.ds(pl.multiple_of(exc * zrows, 16), zrows)
    own_zero = pltpu.make_async_copy(zero_ref, zbuf.at[place], local_sem.at[1])
    own_zero.start()
    zero_copies = [
        pltpu.make_async_remote_copy(
            src_ref=zero_ref,
            dst_ref=zbuf.at[place],
            send_sem=exc_send.at[s],
            recv_sem=exc_recv.at[s],
            device_id={"exc": lax.rem(exc + s, nexc)},
            device_id_type=MESH,
        )
        for s in range(1, nexc)
    ]
    for copy in zero_copies:
        copy.start()
    own_full.wait()
    band_copy.wait()

    go_copies = []
    for g in range(groups):
        row = [None]
        for s in list(range(1, nrow)) + [0]:
            dest = lax.rem(me + s, nrow)
            target = outgo if s else inc
            for v in range(nval):
                at = v % lower * width
                got = jnp.dot(
                    full[v // lower, g, :, at : at + width], sel_ref[g, dest], preferred_element_type=jnp.float32
                )
                target[g, s, :, v * wide : (v + 1) * wide] = got.astype(jnp.bfloat16)
            if s:
                copy = pltpu.make_async_remote_copy(
                    src_ref=outgo.at[g, s],
                    dst_ref=inc.at[g, s],
                    send_sem=go_send.at[g, s],
                    recv_sem=go_recv.at[g, s],
                    device_id={"krow": dest},
                    device_id_type=MESH,
                )
                copy.start()
                row.append(copy)
        go_copies.append(row)

    def contract(write):
        def cols(j, carry):
            at = pl.multiple_of(j * COLS, COLS)
            got = lax.dot_general(
                zbuf[...], table[pl.ds(at, COLS), :], (((1,), (1,)), ((), ())), preferred_element_type=jnp.float32
            )
            write(at, got)
            return carry

        lax.fori_loop(0, table.shape[0] // COLS, cols, 0)

    for g in range(groups):
        build_table(None, None, full.at[:, g], d_ref.at[g], table, modes, nval, ncond, lower)
        if g == 0:
            own_zero.wait()
            for copy in zero_copies:
                copy.wait()

        def first_part(at, got, g=g):
            part[g, :, pl.ds(at, COLS)] = -got

        contract(first_part)

    def neighbour(g, t, out, into, send, recv, device):
        return pltpu.make_async_remote_copy(
            src_ref=out.at[g, t],
            dst_ref=into.at[g, t],
            send_sem=send.at[g, t],
            recv_sem=recv.at[g, t],
            device_id={"krow": device},
            device_id_type=MESH,
        )

    def flow(up):
        if up:
            return me, lambda t: me + nrow - t, lambda g, t: neighbour(
                g, t - 1, up_out, up_in, up_send, up_recv, lax.rem(me + 1, nrow)
            )
        return last - me, lambda t: me - nrow + t, lambda g, t: neighbour(
            g, t - 1, down_out, down_in, down_send, down_recv, lax.rem(me + last, nrow)
        )

    def step(g, t):
        for up in (True, False):
            pos, block, copy = flow(up)
            out, into = (up_out, up_in) if up else (down_out, down_in)

            def mine(block=block):
                d = jnp.clip(block(t), 0, last)
                return part[g, pl.ds(pl.multiple_of(d * kept_pad, 16), kept_pad), :]

            @pl.when(pos == 0)
            def _(out=out, copy=copy, mine=mine):
                out[g, t - 1] = mine().astype(jnp.bfloat16)
                copy(g, t).start()

            if t > 1:

                @pl.when((pos >= 1) & (pos <= t - 1))
                def _(out=out, into=into, copy=copy, mine=mine):
                    copy(g, t - 1).wait_recv()
                    out[g, t - 1] = (mine() + into[g, t - 2].astype(jnp.float32)).astype(jnp.bfloat16)
                    copy(g, t).start()

    def finish(g):
        out_ref[g] = part[g, pl.ds(pl.multiple_of(me * kept_pad, 16), kept_pad), :] * scale
        for up in (True, False):
            pos, _, copy = flow(up)
            into = up_in if up else down_in

            @pl.when(pos >= 1)
            def _(into=into, copy=copy):
                copy(g, last).wait_recv()
                out_ref[g] = out_ref[g] + into[g, last - 1].astype(jnp.float32) * scale

    def elec(g, between):
        for copy in go_copies[g][1:]:
            copy.wait_recv()
        for v in range(nval):
            got = jnp.zeros((x_ref.shape[0], width), jnp.float32)
            for s in range(nrow):
                owner = lax.rem(me + nrow - s, nrow)
                got = got + jnp.dot(
                    inc[g, s, :, v * wide : (v + 1) * wide], perm_ref[g, owner], preferred_element_type=jnp.float32
                )
            x_ref[:, v * width : (v + 1) * width] = got.astype(jnp.bfloat16)
        build_table(x_ref, c_ref.at[g], full.at[:, g], d_ref.at[g], table, modes, nval, ncond, lower)
        between()

        def add_part(at, got):
            part[g, :, pl.ds(at, COLS)] = part[g, :, pl.ds(at, COLS)] + got

        contract(add_part)

    for g in range(groups):

        def between(g=g):
            if g > 0 and nrow > 2:
                step(g - 1, 2)

        elec(g, between)
        step(g, 1)
        if g > 0:
            for t in range(3, nrow):
                step(g - 1, t)
            finish(g - 1)
    for t in range(2, nrow):
        step(groups - 1, t)
    finish(groups - 1)

    for g in range(groups):
        for copy in go_copies[g][1:]:
            copy.wait_send()
        for t in range(1, nrow):
            for up in (True, False):
                pos, _, copy = flow(up)

                @pl.when(pos <= t - 1)
                def _(copy=copy):
                    copy(g, t).wait_send()


def local(coef_zero, coef_shift, coupling, partner):
    nrow = lax.axis_size("krow")
    me = lax.axis_index("krow")
    nband = lax.axis_size("band")
    half = lax.axis_index("band")
    nexc = lax.axis_size("exc")
    mine, nval, ncond, kdev = coef_zero.shape
    nq, share, lower = coef_shift.shape[:3]
    modes = coupling.shape[2]
    cap = kdev // PEERS
    pairs = nval * ncond
    depth = pairs * kdev
    groups = nq // nband
    kept = mine * nexc // nrow
    held = mine // kept
    kept_pad = round_up(kept, ROWS)
    rows = round_up(share, ROWS)
    cols = round_up(modes * rows, COLS)
    scale = (1.0 * pairs * nrow * kdev) ** (-0.5)

    flat = jnp.pad(coef_shift.reshape(nq, share, lower * ncond * kdev), ((0, 0), (0, rows - share), (0, 0)))
    zero = jnp.pad(coef_zero.reshape(held, kept, depth), ((0, 0), (0, kept_pad - kept), (0, 0)))
    zero = zero.reshape(held * kept_pad, depth)

    part = lax.dynamic_slice_in_dim(partner, half * groups, groups, axis=0)
    owner = (part // kdev).reshape(groups, nrow, kdev)
    within = (part % kdev).reshape(groups, nrow, kdev)
    ids = jnp.arange(kdev, dtype=jnp.int32)
    slots = jnp.arange(cap, dtype=jnp.int32)
    tri = (ids[:, None] <= ids[None, :]).astype(jnp.bfloat16)
    eye = jnp.eye(ncond, dtype=jnp.bfloat16)

    def ranked(flags):
        counts = jnp.einsum("qdk,kl->qdl", flags.astype(jnp.bfloat16), tri, preferred_element_type=jnp.float32)
        return flags[..., None] & (counts.astype(jnp.int32)[..., None] - 1 == slots)

    chosen = ranked(owner == me).astype(jnp.bfloat16)
    places = (within[..., None] == ids).astype(jnp.bfloat16)
    select = jnp.einsum("qdkx,qdkj->qdxj", places, chosen, preferred_element_type=jnp.float32).astype(jnp.bfloat16)
    select = (eye[:, None, :, None] * select[:, :, None, :, None, :]).reshape(
        groups, nrow, ncond * kdev, ncond * cap
    )
    my_owner = lax.dynamic_index_in_dim(owner, me, axis=1, keepdims=False)
    match = my_owner[:, None, :] == jnp.arange(nrow, dtype=jnp.int32)[None, :, None]
    perm = jnp.swapaxes(ranked(match), 2, 3).astype(jnp.bfloat16)
    perm = (eye[:, None, :, None] * perm[:, :, None, :, None, :]).reshape(
        groups, nrow, ncond * cap, ncond * kdev
    )

    couple = lax.dynamic_slice_in_dim(coupling, half * groups, groups, axis=1).astype(jnp.float32)
    couple = couple.reshape(2, groups, modes * ncond * ncond, 1, kdev)
    couple = jnp.broadcast_to(couple, couple.shape[:3] + (8, kdev))

    macs = groups * (rows * modes * depth * 4 + 2 * nrow * kept_pad * cols * depth)
    hbm, vmem = pl.BlockSpec(memory_space=pl.ANY), pl.BlockSpec(memory_space=pltpu.VMEM)
    hops = pltpu.VMEM((groups, nrow - 1, kept_pad, cols), jnp.bfloat16)
    parcels = pltpu.VMEM((groups, nrow, rows, pairs * cap), jnp.bfloat16)
    done = pl.pallas_call(
        functools.partial(main_kernel, (modes, nval, ncond, lower, groups, kept_pad, nrow, nexc, scale)),
        out_shape=jax.ShapeDtypeStruct((groups, kept_pad, cols), jnp.float32),
        in_specs=[hbm, hbm, vmem, vmem, vmem, vmem],
        out_specs=vmem,
        scratch_shapes=[
            pltpu.VMEM((nrow * kept_pad, depth), jnp.bfloat16),
            pltpu.VMEM((nband, groups, rows, lower * ncond * kdev), jnp.bfloat16),
            parcels,
            parcels,
            pltpu.VMEM((rows, depth), jnp.bfloat16),
            pltpu.VMEM((cols, depth), jnp.bfloat16),
            pltpu.VMEM((groups, nrow * kept_pad, cols), jnp.float32),
            hops,
            hops,
            hops,
            hops,
            pltpu.SemaphoreType.DMA((2,)),
            pltpu.SemaphoreType.DMA((2,)),
            pltpu.SemaphoreType.DMA((nexc,)),
            pltpu.SemaphoreType.DMA((nexc,)),
        ]
        + [pltpu.SemaphoreType.DMA((groups, nrow))] * 6,
        compiler_params=pltpu.CompilerParams(vmem_limit_bytes=LIMIT, collective_id=0, has_side_effects=True),
        cost_estimate=pl.CostEstimate(flops=2 * macs, bytes_accessed=16 * 2**20, transcendentals=0),
        name="coupling",
    )(zero, flat, select, perm, couple[0], couple[1])
    done = done[:, :kept, : modes * rows].reshape(groups, kept, modes, rows)[..., :share]
    return jnp.swapaxes(done, 0, 1)


def solution(mesh):
    placed = (
        P(("grp", "exc"), None, None, "krow"),
        P(None, ("grp", "exc"), "band", None, "krow"),
        P(None, "grp", None, None, None, "krow"),
        P(),
    )
    return jax.shard_map(
        local,
        mesh=mesh,
        in_specs=placed,
        out_specs=P(("grp", "krow"), "band", None, "exc"),
        check_vma=False,
    )
```

time: 201 us -> 138 us (0.69); the launches traced: 197 us -> 137 us
  Pallas kernels: 48.6 us -> 116 us
  local copies, waits for them, and re-layouts: 64.5 us -> 17 us
  starting transfers between devices: 39.2 us -> 0 us
  waiting for transfers between devices: 29.7 us -> 0 us
  other arithmetic: 14 us -> 3.93 us
    pallas_call x6 -> x1, Pallas kernels: 48.6 us -> 116 us  [local(): pl.pallas_call(functools.partial(main_kernel, (modes, nval, ncond, lower,...]
    ppermute x14 -> x0, starting transfers between devices: 29.7 us -> none  [the longest x6 19.3 us: local(): lax.ppermute(send_up.astype(jnp.bfloat16), 'krow', [(z, z + 1) for z in r...]
    ppermute x14 -> x0, waiting for transfers between devices: 28.2 us -> none  [the longest x6 21.4 us: local(): lax.ppermute(send_up.astype(jnp.bfloat16), 'krow', [(z, z + 1) for z in r...]
    dynamic_slice x14 -> x0, local copies, waits for them, and re-layouts: 24.7 us -> none  [the longest x12 23.7 us: block(): lax.dynamic_index_in_dim(blocks, jnp.clip(d, 0, nrow - 1), axis=0, keepdi...]
    unnamed x80 -> x6, local copies, waits for them, and re-layouts: 22.5 us -> 0.05 us
    all_to_all x2 -> x0, starting transfers between devices: 9.51 us -> none  [local(): lax.all_to_all(outgoing, 'krow', split_axis=0, concat_axis=0, tiled=True)]
    transpose x0 -> x2, local copies, waits for them, and re-layouts: none -> 5.38 us  [local(): return jnp.swapaxes(done, 0, 1)]
    convert_element_type x8 -> x1, other arithmetic: 5.35 us -> 0.94 us  [local(): lax.dynamic_slice_in_dim(coupling, half * groups, groups, axis=1)]
  transfers between devices with their start and end apart: 16 -> 0, of which waited for: 6 -> 0; matrix products, arithmetic and copies ran while one was open for 28% -> 0% of each run, Pallas kernels for 16% -> 0%
where the time goes in v3:
time: 138 us; the launch traced here: 137 us
  Pallas kernels  116 us (84%)
  local copies, waits for them, and re-layouts  17 us (12%)
  other arithmetic  3.93 us (3%)
    pallas_call x1, Pallas kernels, local(): pl.pallas_call(functools.partial(main_kernel, (modes, nval, ncond, lower,...  116 us
    transpose x2, local copies, waits for them, and re-layouts, local(): return jnp.swapaxes(done, 0, 1)  5.38 us

profile of v3, /device:TPU:0, one launch (start us, length us, event | category | flops | bytes accessed | tf_op | source)
XLA Modules:
  0.0 137.3 jit_solution(4515869184501896059)
XLA Ops:
  0.0 0.0 copy-start.1
  0.0 0.1 copy.9
  0.1 0.8 and_select_fusion
  1.0 0.1 fusion
  1.1 0.1 fusion.1
  1.3 0.3 convolution_convert_fusion
  1.6 0.1 mul.44
  1.8 0.1 copy.7
  1.9 0.1 mul.51
  2.0 0.9 dynamic-slice_convert_fusion
  3.0 0.0 copy-done.1
  3.0 0.5 reshape.56
  3.5 1.0 pad.8
  4.5 0.5 mul.54
  5.0 0.4 mul.55
  5.5 1.1 broadcast_multiply_fusion.perm_ref
  6.6 0.5 mul.48
  7.0 0.4 mul.49
  7.5 0.7 copy.8
  8.2 1.1 broadcast_multiply_fusion.1.sel_ref
  9.2 0.0 copy-start
  9.2 1.1 broadcast_in_dim.9.c_ref
  10.3 1.1 broadcast_in_dim.11.d_ref
  11.4 0.0 copy-done
  11.4 1.2 reshape.58
  12.6 1.4 pad.9.flat_ref
  14.0 115.5 %coupling.1 = f32[2,112,1920]{2,1,0:T(8,128)} custom-call(bf16[224,2048]{1,0:T(8,128)(2,1)} %bitcast.29, bf16[4,208,1024]{2,1,0:T(8,128)(2,1)} %pad.9.flat_ref, bf16[2,4,512,128]{3,2,1,0:T(8,128)(2,1)} %broadcast_multiply_fusion.1.sel_ref, bf16[2,4,128,512]{3,2,1,0:T(8,128)(2,1)} %broadcast_multiply_fusion.perm_ref, ...), custom_call_target="tpu_custom_call" | custom-call | flops 14154203136 | bytes 16777216 | tf_op jit(solution)/shard_map/coupling/pallas_call | solution.py:331
  129.5 1.5 %slice.18 = f32[2,100,1872]{2,1,0:T(8,128)S(1)} slice(f32[2,112,1920]{2,1,0:T(8,128)} %coupling.1), slice={[0:2], [0:100], [0:1872]} | slice | bytes 2995200 | tf_op jit(solution)/shard_map/slice | solution.py:358
  131.0 0.8 copy.10
  131.9 1.4 %slice_bitcast_fusion = f32[100,2,9,200]{0,3,2,1:T(8,128)} fusion(f32[2,100,9,208]{1,3,2,0:T(8,128)S(1)} %bitcast.28), kind=kLoop, calls=%fused_computation | loop fusion | bytes 2880000 | tf_op jit(solution)/shard_map/transpose | solution.py:359
  133.3 4.0 %copy.11 = f32[100,2,9,200]{3,1,2,0:T(2,128)} copy(f32[100,2,9,200]{0,3,2,1:T(8,128)} %slice_bitcast_fusion) | data formatting | bytes 2880000 | tf_op jit(solution)/shard_map/transpose | solution.py:359
  (10 shorter events, 0.2 us)
Async XLA Ops:
  0.0 3.0 %copy-start.1 = (bf16[200,4,4,128]{3,2,1,0:T(4,128)(2,1)S(1)}, bf16[200,4,4,128]{3,2,1,0:T(4,128)(2,1)}, u32[]{:S(2)}) copy-start(bf16[200,4,4,128]{3,2,1,0:T(4,128)(2,1)} %param.4) | copy-start | bytes 2457604
  9.2 2.2 %copy-start = (bf16[4,200,2,4,128]{4,3,2,1,0:T(4,128)(2,1)S(1)}, bf16[4,200,2,4,128]{4,3,2,1,0:T(4,128)(2,1)}, u32[]{:S(2)}) copy-start(bf16[4,200,2,4,128]{4,3,2,1,0:T(4,128)(2,1)} %param.5) | copy-start | bytes 4915204

commit v4 on v3

--- a/solution.py
+++ b/solution.py
@@ -76,11 +76,11 @@
 
 
 def main_kernel(
-    dims, zero_ref, flat_ref, sel_ref, perm_ref, c_ref, d_ref, out_ref,
-    zbuf, full, outgo, inc, x_ref, table, part, up_out, up_in, down_out, down_in,
+    dims, zero_ref, flat_ref, sel_small, perm_small, c_small, d_small, out_ref,
+    sel_ref, perm_ref, c_ref, d_ref, zbuf, full, outgo, inc, x_ref, table, part, up_out, up_in, down_out, down_in,
     local_sem, band_sem, exc_send, exc_recv, go_send, go_recv, up_send, up_recv, down_send, down_recv,
 ):
-    modes, nval, ncond, lower, groups, kept_pad, nrow, nexc, scale = dims
+    modes, nval, ncond, lower, groups, kept_pad, share, nrow, nexc, scale = dims
     me, exc, half = lax.axis_index("krow"), lax.axis_index("exc"), lax.axis_index("band")
     width, wide = sel_ref.shape[2:]
     zrows = zero_ref.shape[0]
@@ -121,6 +121,26 @@
     ]
     for copy in zero_copies:
         copy.start()
+    sel_ref[...] = jnp.zeros(sel_ref.shape, sel_ref.dtype)
+    perm_ref[...] = jnp.zeros(perm_ref.shape, perm_ref.dtype)
+    tall, thin = sel_small.shape[2:]
+    for g in range(groups):
+        for d in range(nrow):
+            for c in range(ncond):
+                long, short = slice(c * tall, (c + 1) * tall), slice(c * thin, (c + 1) * thin)
+                sel_ref[g, d, long, short] = sel_small[g, d]
+                perm_ref[g, d, short, long] = perm_small[g, d]
+
+        def spread(i, carry, g=g):
+            c_ref[g, i] = jnp.broadcast_to(c_small[g, pl.ds(i, 1), :], c_ref.shape[2:])
+            d_ref[g, i] = jnp.broadcast_to(d_small[g, pl.ds(i, 1), :], d_ref.shape[2:])
+            return carry
+
+        lax.fori_loop(0, c_small.shape[1], spread, 0)
+    chunks = table.shape[0] // COLS
+    used = chunks * kept_pad
+    if used < part.shape[2]:
+        part[:, :, used:, :] = jnp.zeros(part.shape[:2] + (part.shape[2] - used, COLS), jnp.float32)
     own_full.wait()
     band_copy.wait()
 
@@ -155,10 +175,11 @@
             got = lax.dot_general(
                 zbuf[...], table[pl.ds(at, COLS), :], (((1,), (1,)), ((), ())), preferred_element_type=jnp.float32
             )
-            write(at, got)
+            for d in range(nrow):
+                write(d, pl.ds(pl.multiple_of(j * kept_pad, 8), kept_pad), got[d * kept_pad : (d + 1) * kept_pad])
             return carry
 
-        lax.fori_loop(0, table.shape[0] // COLS, cols, 0)
+        lax.fori_loop(0, chunks, cols, 0)
 
     for g in range(groups):
         build_table(None, None, full.at[:, g], d_ref.at[g], table, modes, nval, ncond, lower)
@@ -167,8 +188,8 @@
             for copy in zero_copies:
                 copy.wait()
 
-        def first_part(at, got, g=g):
-            part[g, :, pl.ds(at, COLS)] = -got
+        def first_part(d, at, got, g=g):
+            part[g, d, at, :] = -got
 
         contract(first_part)
 
@@ -197,8 +218,7 @@
             out, into = (up_out, up_in) if up else (down_out, down_in)
 
             def mine(block=block):
-                d = jnp.clip(block(t), 0, last)
-                return part[g, pl.ds(pl.multiple_of(d * kept_pad, 16), kept_pad), :]
+                return part[g, jnp.clip(block(t), 0, last)]
 
             @pl.when(pos == 0)
             def _(out=out, copy=copy, mine=mine):
@@ -214,7 +234,6 @@
                     copy(g, t).start()
 
     def finish(g):
-        out_ref[g] = part[g, pl.ds(pl.multiple_of(me * kept_pad, 16), kept_pad), :] * scale
         for up in (True, False):
             pos, _, copy = flow(up)
             into = up_in if up else down_in
@@ -222,7 +241,14 @@
             @pl.when(pos >= 1)
             def _(into=into, copy=copy):
                 copy(g, last).wait_recv()
-                out_ref[g] = out_ref[g] + into[g, last - 1].astype(jnp.float32) * scale
+                part[g, me] = part[g, me] + into[g, last - 1].astype(jnp.float32)
+
+        total = jnp.concatenate(
+            [part[g, me, j * kept_pad : (j + 1) * kept_pad, :] for j in range(chunks)], axis=1
+        )
+        rows = x_ref.shape[0]
+        for m in range(modes):
+            out_ref[g, m] = total[:, m * rows : m * rows + share] * scale
 
     def elec(g, between):
         for copy in go_copies[g][1:]:
@@ -238,8 +264,8 @@
         build_table(x_ref, c_ref.at[g], full.at[:, g], d_ref.at[g], table, modes, nval, ncond, lower)
         between()
 
-        def add_part(at, got):
-            part[g, :, pl.ds(at, COLS)] = part[g, :, pl.ds(at, COLS)] + got
+        def add_part(d, at, got):
+            part[g, d, at, :] = part[g, d, at, :] + got
 
         contract(add_part)
 
@@ -286,7 +312,8 @@
     groups = nq // nband
     kept = mine * nexc // nrow
     held = mine // kept
-    kept_pad = round_up(kept, ROWS)
+    kept_pad = round_up(kept, 8)
+    wire = round_up(kept_pad * (round_up(modes * round_up(share, ROWS), COLS) // COLS), ROWS)
     rows = round_up(share, ROWS)
     cols = round_up(modes * rows, COLS)
     scale = (1.0 * pairs * nrow * kdev) ** (-0.5)
@@ -301,7 +328,6 @@
     ids = jnp.arange(kdev, dtype=jnp.int32)
     slots = jnp.arange(cap, dtype=jnp.int32)
     tri = (ids[:, None] <= ids[None, :]).astype(jnp.bfloat16)
-    eye = jnp.eye(ncond, dtype=jnp.bfloat16)
 
     def ranked(flags):
         counts = jnp.einsum("qdk,kl->qdl", flags.astype(jnp.bfloat16), tri, preferred_element_type=jnp.float32)
@@ -310,37 +336,34 @@
     chosen = ranked(owner == me).astype(jnp.bfloat16)
     places = (within[..., None] == ids).astype(jnp.bfloat16)
     select = jnp.einsum("qdkx,qdkj->qdxj", places, chosen, preferred_element_type=jnp.float32).astype(jnp.bfloat16)
-    select = (eye[:, None, :, None] * select[:, :, None, :, None, :]).reshape(
-        groups, nrow, ncond * kdev, ncond * cap
-    )
     my_owner = lax.dynamic_index_in_dim(owner, me, axis=1, keepdims=False)
     match = my_owner[:, None, :] == jnp.arange(nrow, dtype=jnp.int32)[None, :, None]
     perm = jnp.swapaxes(ranked(match), 2, 3).astype(jnp.bfloat16)
-    perm = (eye[:, None, :, None] * perm[:, :, None, :, None, :]).reshape(
-        groups, nrow, ncond * cap, ncond * kdev
-    )
-
     couple = lax.dynamic_slice_in_dim(coupling, half * groups, groups, axis=1).astype(jnp.float32)
-    couple = couple.reshape(2, groups, modes * ncond * ncond, 1, kdev)
-    couple = jnp.broadcast_to(couple, couple.shape[:3] + (8, kdev))
+    couple = couple.reshape(2, groups, modes * ncond * ncond, kdev)
+    spread = pltpu.VMEM((groups, modes * ncond * ncond, 8, kdev), jnp.float32)
 
     macs = groups * (rows * modes * depth * 4 + 2 * nrow * kept_pad * cols * depth)
     hbm, vmem = pl.BlockSpec(memory_space=pl.ANY), pl.BlockSpec(memory_space=pltpu.VMEM)
-    hops = pltpu.VMEM((groups, nrow - 1, kept_pad, cols), jnp.bfloat16)
+    hops = pltpu.VMEM((groups, nrow - 1, wire, COLS), jnp.bfloat16)
     parcels = pltpu.VMEM((groups, nrow, rows, pairs * cap), jnp.bfloat16)
     done = pl.pallas_call(
-        functools.partial(main_kernel, (modes, nval, ncond, lower, groups, kept_pad, nrow, nexc, scale)),
-        out_shape=jax.ShapeDtypeStruct((groups, kept_pad, cols), jnp.float32),
+        functools.partial(main_kernel, (modes, nval, ncond, lower, groups, kept_pad, share, nrow, nexc, scale)),
+        out_shape=jax.ShapeDtypeStruct((groups, modes, kept_pad, share), jnp.float32),
         in_specs=[hbm, hbm, vmem, vmem, vmem, vmem],
         out_specs=vmem,
         scratch_shapes=[
+            pltpu.VMEM((groups, nrow, ncond * kdev, ncond * cap), jnp.bfloat16),
+            pltpu.VMEM((groups, nrow, ncond * cap, ncond * kdev), jnp.bfloat16),
+            spread,
+            spread,
             pltpu.VMEM((nrow * kept_pad, depth), jnp.bfloat16),
             pltpu.VMEM((nband, groups, rows, lower * ncond * kdev), jnp.bfloat16),
             parcels,
             parcels,
             pltpu.VMEM((rows, depth), jnp.bfloat16),
             pltpu.VMEM((cols, depth), jnp.bfloat16),
-            pltpu.VMEM((groups, nrow * kept_pad, cols), jnp.float32),
+            pltpu.VMEM((groups, nrow, wire, COLS), jnp.float32),
             hops,
             hops,
             hops,
@@ -355,8 +378,7 @@
         cost_estimate=pl.CostEstimate(flops=2 * macs, bytes_accessed=16 * 2**20, transcendentals=0),
         name="coupling",
     )(zero, flat, select, perm, couple[0], couple[1])
-    done = done[:, :kept, : modes * rows].reshape(groups, kept, modes, rows)[..., :share]
-    return jnp.swapaxes(done, 0, 1)
+    return jnp.transpose(done[:, :, :kept], (2, 0, 1, 3))
 
 
 def solution(mesh):

time: 138 us -> 123 us (0.89)
  local copies, waits for them, and re-layouts: 17 us -> 9.54 us
  Pallas kernels: 116 us -> 110 us
  other arithmetic: 3.93 us -> 2.39 us
    pallas_call x1, Pallas kernels: 116 us -> 110 us  [local(): pl.pallas_call(functools.partial(main_kernel, (modes, nval, ncond, lower,...]
    mul x8 -> x0, local copies, waits for them, and re-layouts: 2.82 us -> none  [the longest x5 1.8 us: local(): eye[:, None, :, None] * select[:, :, None, :, None, :]]
    slice x2 -> x0, local copies, waits for them, and re-layouts: 2.35 us -> none  [local(): done[:, :kept, :modes * rows].reshape(groups, kept, modes, rows)]
    broadcast_in_dim x2 -> x0, local copies, waits for them, and re-layouts: 2.19 us -> none  [local(): couple = jnp.broadcast_to(couple, couple.shape[:3] + (8, kdev))]
    mul x2 -> x0, other arithmetic: 2.16 us -> none  [the longest x1 1.1 us: local(): eye[:, None, :, None] * perm[:, :, None, :, None, :]]
    transpose x2, local copies, waits for them, and re-layouts: 5.38 us -> 3.83 us  [local(): return jnp.transpose(done[:, :, :kept], (2, 0, 1, 3))]
where the time goes in v4:
time: 123 us
  Pallas kernels  110 us (89%)
  local copies, waits for them, and re-layouts  9.54 us (8%)
  other arithmetic  2.39 us (2%)
    pallas_call x1, Pallas kernels, local(): pl.pallas_call(functools.partial(main_kernel, (modes, nval, ncond, lower,...  110 us
    transpose x2, local copies, waits for them, and re-layouts, local(): return jnp.transpose(done[:, :, :kept], (2, 0, 1, 3))  3.83 us

profile of v4, /device:TPU:0, one launch (start us, length us, event | category | flops | bytes accessed | tf_op | source)
XLA Modules:
  0.0 122.5 jit_solution(410310657915440568)
XLA Ops:
  0.0 0.0 copy-start.1
  0.0 0.8 and_select_fusion
  0.9 0.1 fusion
  1.0 0.1 fusion.1
  1.2 0.3 convolution_convert_fusion
  1.5 0.7 fusion.6.perm_small
  2.1 0.9 copy.9.sel_small
  3.0 0.9 dynamic-slice_convert_fusion
  3.9 0.0 copy-start
  3.9 0.8 fusion.12
  4.7 0.0 copy-done.1
  4.7 0.5 reshape.30
  5.2 1.0 pad.8
  6.2 0.0 copy-done
  6.2 1.2 reshape.32
  7.4 1.4 %pad.9.flat_ref = bf16[4,208,1024]{2,1,0:T(8,128)(2,1)} pad(bf16[4,200,1024]{2,1,0:T(8,128)(2,1)S(1)} %reshape.32, bf16[]{:T(256)} %constant.39.clone.1), padding=0_0x0_8x0_0 | pad | bytes 3342338 | tf_op jit(solution)/shard_map/jit(_pad)/pad | solution.py:321
  8.8 109.9 %coupling.1 = f32[2,9,104,200]{3,2,1,0:T(8,128)} custom-call(bf16[208,2048]{1,0:T(8,128)(2,1)} %bitcast.13, bf16[4,208,1024]{2,1,0:T(8,128)(2,1)} %pad.9.flat_ref, bf16[2,4,128,32]{3,2,1,0:T(8,128)(2,1)} %copy.9.sel_small, bf16[2,4,32,128]{3,2,1,0:T(8,128)(2,1)} %fusion.6.perm_small, f32[2,144,128]{2,1,0:T(8,128)} %bitcast.15, f32[2,144,128]{2,1,0:T(8,128)} %bitcast.14), custom_call_target="tpu_custom_call" | custom-call | flops 13147570176 | bytes 16777216 | tf_op jit(solution)/shard_map/coupling/pallas_call | solution.py:350
  118.7 1.7 %slice_bitcast_fusion = f32[100,2,9,200]{3,0,2,1:T(8,128)S(1)} fusion(f32[2,9,104,200]{3,2,1,0:T(8,128)} %coupling.1), kind=kLoop, calls=%fused_computation | loop fusion | bytes 2880000 | tf_op jit(solution)/shard_map/transpose | solution.py:381
  120.3 2.2 %copy.10 = f32[100,2,9,200]{3,1,2,0:T(2,128)} copy(f32[100,2,9,200]{3,0,2,1:T(8,128)S(1)} %slice_bitcast_fusion) | data formatting | bytes 2880000 | tf_op jit(solution)/shard_map/transpose | solution.py:381
  (5 shorter events, 0.1 us)
Async XLA Ops:
  0.0 4.7 %copy-start.1 = (bf16[200,4,4,128]{3,2,1,0:T(4,128)(2,1)S(1)}, bf16[200,4,4,128]{3,2,1,0:T(4,128)(2,1)}, u32[]{:S(2)}) copy-start(bf16[200,4,4,128]{3,2,1,0:T(4,128)(2,1)} %param.4) | copy-start | bytes 2457604
  3.9 2.3 %copy-start = (bf16[4,200,2,4,128]{4,3,2,1,0:T(4,128)(2,1)S(1)}, bf16[4,200,2,4,128]{4,3,2,1,0:T(4,128)(2,1)}, u32[]{:S(2)}) copy-start(bf16[4,200,2,4,128]{4,3,2,1,0:T(4,128)(2,1)} %param.5) | copy-start | bytes 4915204

commit v5 on v4

--- a/solution.py
+++ b/solution.py
@@ -220,17 +220,21 @@
             def mine(block=block):
                 return part[g, jnp.clip(block(t), 0, last)]
 
-            @pl.when(pos == 0)
-            def _(out=out, copy=copy, mine=mine):
-                out[g, t - 1] = mine().astype(jnp.bfloat16)
+            @pl.when((pos >= 1) & (pos <= t - 1))
+            def _(out=out, into=into, copy=copy, mine=mine):
+                copy(g, t - 1).wait_recv()
+                out[g, t - 1] = (mine() + into[g, t - 2].astype(jnp.float32)).astype(jnp.bfloat16)
                 copy(g, t).start()
 
-            if t > 1:
-
-                @pl.when((pos >= 1) & (pos <= t - 1))
-                def _(out=out, into=into, copy=copy, mine=mine):
-                    copy(g, t - 1).wait_recv()
-                    out[g, t - 1] = (mine() + into[g, t - 2].astype(jnp.float32)).astype(jnp.bfloat16)
+    def ends(g):
+        for t in range(1, nrow):
+            for up in (True, False):
+                pos, block, copy = flow(up)
+                out = up_out if up else down_out
+
+                @pl.when(pos == 0)
+                def _(out=out, block=block, copy=copy):
+                    out[g, t - 1] = part[g, jnp.clip(block(t), 0, last)].astype(jnp.bfloat16)
                     copy(g, t).start()
 
     def finish(g):
@@ -276,13 +280,18 @@
                 step(g - 1, 2)
 
         elec(g, between)
-        step(g, 1)
+        ends(g)
         if g > 0:
             for t in range(3, nrow):
                 step(g - 1, t)
-            finish(g - 1)
+            if g < groups - 1:
+                finish(g - 1)
     for t in range(2, nrow):
         step(groups - 1, t)
+        if t == 2 and groups > 1:
+            finish(groups - 2)
+    if nrow == 2 and groups > 1:
+        finish(groups - 2)
     finish(groups - 1)
 
     for g in range(groups):

time: 123 us -> 122 us (level)
  no operation moved by 1% of the time
where the time goes in v5:
time: 122 us; the launch traced here: 121 us
  Pallas kernels  109 us (89%)
  local copies, waits for them, and re-layouts  9.54 us (8%)
  other arithmetic  2.39 us (2%)
    pallas_call x1, Pallas kernels, local(): pl.pallas_call(functools.partial(main_kernel, (modes, nval, ncond, lower,...  109 us
    transpose x2, local copies, waits for them, and re-layouts, local(): return jnp.transpose(done[:, :, :kept], (2, 0, 1, 3))  3.83 us

profile of v5, /device:TPU:0, one launch (start us, length us, event | category | flops | bytes accessed | tf_op | source)
XLA Modules:
  0.0 121.4 jit_solution(12361711474827065157)
XLA Ops:
  0.0 0.0 copy-start.1
  0.0 0.8 and_select_fusion
  0.9 0.1 fusion
  1.0 0.1 fusion.1
  1.2 0.3 convolution_convert_fusion
  1.5 0.7 fusion.6.perm_small
  2.1 0.9 copy.9.sel_small
  3.0 0.9 dynamic-slice_convert_fusion
  3.9 0.0 copy-start
  3.9 0.8 fusion.12
  4.7 0.0 copy-done.1
  4.7 0.5 reshape.30
  5.2 1.0 pad.8
  6.2 0.0 copy-done
  6.2 1.2 reshape.32
  7.4 1.4 %pad.9.flat_ref = bf16[4,208,1024]{2,1,0:T(8,128)(2,1)} pad(bf16[4,200,1024]{2,1,0:T(8,128)(2,1)S(1)} %reshape.32, bf16[]{:T(256)} %constant.39.clone.1), padding=0_0x0_8x0_0 | pad | bytes 3342338 | tf_op jit(solution)/shard_map/jit(_pad)/pad | solution.py:330
  8.8 108.8 %coupling.1 = f32[2,9,104,200]{3,2,1,0:T(8,128)} custom-call(bf16[208,2048]{1,0:T(8,128)(2,1)} %bitcast.13, bf16[4,208,1024]{2,1,0:T(8,128)(2,1)} %pad.9.flat_ref, bf16[2,4,128,32]{3,2,1,0:T(8,128)(2,1)} %copy.9.sel_small, bf16[2,4,32,128]{3,2,1,0:T(8,128)(2,1)} %fusion.6.perm_small, f32[2,144,128]{2,1,0:T(8,128)} %bitcast.15, f32[2,144,128]{2,1,0:T(8,128)} %bitcast.14), custom_call_target="tpu_custom_call" | custom-call | flops 13147570176 | bytes 16777216 | tf_op jit(solution)/shard_map/coupling/pallas_call | solution.py:359
  117.5 1.7 %slice_bitcast_fusion = f32[100,2,9,200]{3,0,2,1:T(8,128)S(1)} fusion(f32[2,9,104,200]{3,2,1,0:T(8,128)} %coupling.1), kind=kLoop, calls=%fused_computation | loop fusion | bytes 2880000 | tf_op jit(solution)/shard_map/transpose | solution.py:390
  119.2 2.2 %copy.10 = f32[100,2,9,200]{3,1,2,0:T(2,128)} copy(f32[100,2,9,200]{3,0,2,1:T(8,128)S(1)} %slice_bitcast_fusion) | data formatting | bytes 2880000 | tf_op jit(solution)/shard_map/transpose | solution.py:390
  (5 shorter events, 0.1 us)
Async XLA Ops:
  0.0 4.7 %copy-start.1 = (bf16[200,4,4,128]{3,2,1,0:T(4,128)(2,1)S(1)}, bf16[200,4,4,128]{3,2,1,0:T(4,128)(2,1)}, u32[]{:S(2)}) copy-start(bf16[200,4,4,128]{3,2,1,0:T(4,128)(2,1)} %param.4) | copy-start | bytes 2457604
  3.9 2.3 %copy-start = (bf16[4,200,2,4,128]{4,3,2,1,0:T(4,128)(2,1)S(1)}, bf16[4,200,2,4,128]{4,3,2,1,0:T(4,128)(2,1)}, u32[]{:S(2)}) copy-start(bf16[4,200,2,4,128]{4,3,2,1,0:T(4,128)(2,1)} %param.5) | copy-start | bytes 4915204
